TPU v7x, 128 devices: a whole 4x4x4 slice. The times are simulated.
128 devices in a mesh: row: 4 (over y_lo, core), feat: 32 (over y_hi, z, x).
Axes of the slice: x: 4, y: 4 (y_hi: 2, y_lo: 2; y = y_hi * 2 + y_lo), z: 4, core: 2. Of those that a mesh axis runs over, the one named last changes fastest.
Arguments:
- activations: float32 [4, 4096, 4096], P(None, ('row', 'feat')), may hold values from -6 to 6
- out_grads: float32 [4, 4096, 4096], P(None, ('row', 'feat')), may hold values from -6 to 6
- proj_in: float32 [4096, 128], replicated, may hold values from -0.09375 to 0.09375
- proj_out: float32 [4096, 128], replicated, may hold values from -0.09375 to 0.09375
- inv_in: float32 [4, 128, 128], replicated, may hold values from -0.3 to 2, as said below
- inv_out: float32 [4, 128, 128], replicated, may hold values from -0.3 to 2, as said below
- stored: float32 [8192, 4, 16384], P('row', None, 'feat'), may hold values from -0.00390625 to 0.00390625
- query_order: int32 [128], replicated, may hold values from 0 to 127, each once
Outputs:
- scores: float32 [128, 8192], P('feat', 'row')
Inputs may be any that keep to these rules, and one draw needn't show every extreme that they name: `query_order`: each query appears exactly once. `inv_in`: square matrices. `inv_out`: square matrices.
All inputs are finite; a program needn't handle non-finite values.
Results may differ from a plain program's by a relative error of at most 0.0001.
Values sent between devices are 32-bit elements; how exact they have to be, the bound alone decides.
No kernel may reach another device: no remote copies, remote signals or barrier semaphores. Data moves between devices by JAX's collectives and lax.ppermute only.
A program may use at most 128 MiB of HBM per device.

v0:
```python
import jax
import jax.numpy as jnp
from jax import lax
from jax.sharding import PartitionSpec as P

TOK = 32


def per_device(activations, out_grads, proj_in, proj_out, inv_in, inv_out, stored, query_order):
    highest = lax.Precision.HIGHEST
    feat_idx = lax.axis_index("feat")
    layer_count = inv_in.shape[0]
    low_rank = inv_in.shape[1]
    q_dev = activations.shape[1] // TOK
    slice_len = stored.shape[2]
    acts_low = jnp.einsum("ltd,dr->ltr", activations, proj_in, precision=highest)
    grads_low = jnp.einsum("ltd,dr->ltr", out_grads, proj_out, precision=highest)
    acts_four = acts_low.reshape(layer_count, q_dev, TOK, low_rank)
    grads_four = grads_low.reshape(layer_count, q_dev, TOK, low_rank)
    gradient = jnp.einsum("lqti,lqtj->lqij", grads_four, acts_four, precision=highest)
    left_side = jnp.einsum("lik,lqkj->lqij", inv_out, gradient, precision=highest)
    precond = jnp.einsum("lqik,lkj->qlij", left_side, inv_in, precision=highest)
    flat_grads = precond.reshape(q_dev, layer_count, low_rank * low_rank)
    gathered = lax.all_gather(flat_grads, ("row", "feat"), axis=0, tiled=True)
    my_slice = lax.dynamic_slice_in_dim(gathered, feat_idx * slice_len, slice_len, 2)
    picked = jnp.take(my_slice, query_order, axis=0)
    return lax.psum_scatter(
        jnp.einsum("qlf,slf->qs", picked, stored, precision=highest),
        "feat",
        scatter_dimension=0,
        tiled=True,
    )


def solution(mesh):
    placed = (
        P(None, ("row", "feat"), None),
        P(None, ("row", "feat"), None),
        P(),
        P(),
        P(),
        P(),
        P("row", None, "feat"),
        P(),
    )
    return jax.shard_map(
        per_device, mesh=mesh, in_specs=placed, out_specs=P("feat", "row"), check_vma=False
    )
```

profile of v0, /device:TPU:0, one launch (start us, length us, event | category | flops | bytes accessed | tf_op | source)
XLA Modules:
  0.0 757.4 jit_solution(1823423268811914839)
XLA Ops:
  6.5 0.0 copy-start
  6.5 0.0 all-gather.2.cloned.1.call-start
  6.5 1.6 copy-done
  8.1 0.0 copy-start.1
  8.1 0.0 copy-start.2
  8.1 3.9 fusion.5
  12.0 0.0 copy-done.1
  12.0 0.0 copy-done.2
  12.0 0.0 copy-start.3
  12.1 0.0 copy-start.4
  12.1 2.2 fusion.7
  14.2 0.0 copy-start.5
  14.2 0.6 fusion.10
  14.8 0.0 copy-done.3
  14.8 0.7 convolution_bitcast_fusion.1
  15.5 0.0 copy-done.4
  15.5 0.6 convolution_bitcast_fusion
  16.1 0.8 reshape.23
  17.0 0.0 all-gather.2.cloned.1.call-update
  17.0 0.0 all-reduce.3.cloned.1.call-start
  17.1 0.0 copy-done.5
  17.1 351.0 %all-gather.2.cloned.1.call-done = f32[128,4,16384]{2,1,0:T(4,128)} async-done(((f32[1,4,16384]{2,1,0:T(4,128)}), f32[128,4,16384]{2,1,0:T(4,128)}) %all-gather.2.cloned.1.call-update) | async-done | bytes 33554448 | tf_op jit(solution)/shard_map/all_gather | solution.py:24
  368.1 1.3 constant_dynamic-slice_fusion.1
  369.4 2.1 gather_fusion
  371.4 1.5 broadcast_select_fusion
  373.0 0.0 copy-start.6
  373.0 22.1 %fusion.2 = f32[128,2048]{1,0:T(8,128)} fusion(f32[2048,4,512]{2,1,0:T(4,128)} %param.14, f32[128,4,512]{2,1,0:T(4,128)S(1)} %broadcast_select_fusion), kind=kOutput, calls=%fused_computation.3 | convolution fusion | flops 6442450944 | bytes 18874368 | tf_op jit(solution)/shard_map/qlf,slf->qs/dot_general | solution.py:28
  395.1 0.0 all-reduce.3.cloned.1.call-update
  395.2 0.0 copy-done.6
  395.2 0.6 dynamic-slice
  396.4 352.7 %all-reduce.3.cloned.1.call-done = f32[128,2048]{1,0:T(8,128)} async-done(((f32[128,2048]{1,0:T(8,128)}), f32[128,2048]{1,0:T(8,128)}) %all-reduce.3.cloned.1.call-update) | async-done | bytes 1048592
  749.1 1.5 constant_dynamic-slice_fusion
  (3 shorter events, 0.0 us)
Async XLA Ops:
  6.5 1.6 copy-start
  6.5 361.5 %all-gather.2.cloned.1.call-start = ((), (), s32[]{:S(2)}) async-start(), calls=%async_computation | async-start | bytes 33816576 | tf_op jit(solution)/shard_map/all_gather | solution.py:24
  8.1 3.9 copy-start.1
  8.1 3.9 copy-start.2
  12.0 2.8 copy-start.3
  12.1 3.5 copy-start.4
  14.2 2.8 copy-start.5
  17.0 732.1 %all-reduce.3.cloned.1.call-start = ((), (), s32[]{:S(2)}) async-start(), calls=%async_computation.1 | async-start | bytes 2097152
  373.0 22.2 %copy-start.6 = (u32[128]{0:T(128)S(1)}, u32[128]{0:T(128)}, u32[]{:S(2)}) copy-start(u32[128]{0:T(128)} %constant.29) | copy-start | bytes 1540
Sparse Core Ops, SparseCore 0:
  17.1 350.8 all-gather.1
  395.3 353.7 all-reduce.2
where the time goes:
time: 758 us; the launch traced here: 757 us
  waiting for transfers between devices  704 us (93%)
  matrix products  30 us (4%)
  between operations  14.2 us (2%)
  local copies, waits for them, and re-layouts  7.89 us (1%)
    unnamed x3, waiting for transfers between devices  353 us
    all_gather x1, waiting for transfers between devices, per_device(): gathered = lax.all_gather(flat_grads, ('row', 'feat'), axis=0, tiled=True)  351 us
    dot_general x1, matrix products, per_device(): jnp.einsum('qlf,slf->qs', picked, stored, precision=highest)  22.1 us
  transfers between devices with their start and end apart: 2, of which 2 were waited for; matrix products, arithmetic and copies ran while one was open for 0% of the time, Pallas kernels for 0%

commit v1 on v0

v1 whole, which is shorter than its diff:
```python
import functools

import jax
import jax.numpy as jnp
from jax import lax
from jax.experimental import pallas as pl
from jax.experimental.pallas import tpu as pltpu
from jax.sharding import PartitionSpec as P

TOK = 32
F32, BF16 = jnp.float32, jnp.bfloat16
NN = (((1,), (0,)), ((), ()))
NT = (((1,), (1,)), ((), ()))
TN = (((0,), (0,)), ((), ()))
MIB = 1024 * 1024
WHOLE = pl.BlockSpec(memory_space=pltpu.VMEM)


def limit(mib):
    return pltpu.CompilerParams(vmem_limit_bytes=mib * MIB)


def near(x):
    return pltpu.with_memory_space_constraint(x, pltpu.VMEM)


def far(x):
    return pltpu.with_memory_space_constraint(x, pltpu.HBM)


def dot(a, b, dims=NN):
    return lax.dot_general(a, b, dims, preferred_element_type=F32)


def exact_dot(a, b, dims=NN):
    return lax.dot_general(a, b, dims, precision=lax.Precision.HIGHEST, preferred_element_type=F32)


def pieces(x):
    high = x.astype(BF16)
    return high, (x - high.astype(F32)).astype(BF16)


def wide_product(x, w):
    rows, cols = x.shape[0], w.shape[1]
    both = dot(jnp.concatenate(pieces(x), axis=0), jnp.concatenate(pieces(w), axis=1))
    return (both[rows:, cols:] + both[rows:, :cols]) + both[:rows, cols:] + both[:rows, :cols]


def precond_kernel(acts_ref, grads_ref, pin_ref, pout_ref, iin_ref, iout_ref, out_ref, acts_sum, grads_sum):
    step = pl.program_id(0)
    layers, tok, width = acts_ref.shape
    rank = pin_ref.shape[1]
    acts = wide_product(acts_ref[...].reshape(layers * tok, width), pin_ref[...])
    grads = wide_product(grads_ref[...].reshape(layers * tok, width), pout_ref[...])

    @pl.when(step == 0)
    def _():
        acts_sum[...] = acts
        grads_sum[...] = grads

    @pl.when(step > 0)
    def _():
        acts_sum[...] += acts
        grads_sum[...] += grads

    @pl.when(step == pl.num_programs(0) - 1)
    def _():
        rows, slices, per, _ = out_ref.shape
        per = per // layers
        for l in range(layers):
            mine = slice(l * tok, (l + 1) * tok)
            right = exact_dot(acts_sum[mine, :], iin_ref[l])
            left = exact_dot(grads_sum[mine, :], iout_ref[l], NT)
            cond = exact_dot(left, right, TN).reshape(slices, per, rank)
            for r in range(rows):
                out_ref[r, :, l * per : (l + 1) * per, :] = cond


def preconditioned(activations, out_grads, proj_in, proj_out, inv_in, inv_out, rows, slices, block=1024):
    layers, tok, width = activations.shape
    rank = proj_in.shape[1]
    per = rank // slices
    tokens = pl.BlockSpec((layers, tok, block), lambda k: (0, 0, k))
    side = pl.BlockSpec((block, rank), lambda k: (k, 0))
    return pl.pallas_call(
        precond_kernel,
        grid=(width // block,),
        in_specs=[tokens, tokens, side, side, WHOLE, WHOLE],
        out_specs=WHOLE,
        out_shape=pltpu.VMEM((rows, slices, layers * per, rank), F32),
        scratch_shapes=[pltpu.VMEM((layers * tok, rank), F32)] * 2,
        compiler_params=limit(8),
        name="precond",
    )(far(activations), far(out_grads), far(proj_in), far(proj_out), inv_in, inv_out)


def split_kernel(stored_ref, high_ref, low_ref):
    rows, layers, width = stored_ref.shape
    for l in range(layers):
        cols = slice(l * width, (l + 1) * width)
        high_ref[:, cols], low_ref[:, cols] = pieces(stored_ref[:, l, :])


def split_stored(stored, block=256):
    store, layers, width = stored.shape
    half = pl.BlockSpec((block, layers * width), lambda s: (s, 0))
    return pl.pallas_call(
        split_kernel,
        grid=(store // block,),
        in_specs=[pl.BlockSpec((block, layers, width), lambda s: (s, 0, 0))],
        out_specs=[half, half],
        out_shape=[pltpu.HBM((store, layers * width), BF16)] * 2,
        compiler_params=limit(16),
        cost_estimate=pl.CostEstimate(flops=stored.size * 8, bytes_accessed=stored.size * 8, transcendentals=0),
        name="split_stored",
    )(far(stored))


def scores_kernel(recv_ref, order_ref, high_ref, low_ref, out_ref, picked):
    queries, per, rank = recv_ref.shape
    slices, sub, half = out_ref.shape
    group = queries // slices
    tile = high_ref.shape[0]
    step = pl.program_id(0)

    @pl.when(step == 0)
    def _():
        ids = lax.broadcasted_iota(jnp.int32, (queries, queries), 0)
        chosen = (ids == order_ref[...]).astype(F32).astype(BF16)
        for t in range(per):
            cols = slice(t * rank, (t + 1) * rank)
            both = dot(chosen, jnp.concatenate(pieces(recv_ref[:, t, :]), axis=1), TN)
            picked[:queries, cols] = both[:, :rank].astype(BF16)
            picked[queries:, cols] = both[:, rank:].astype(BF16)

    wide = dot(picked[...], high_ref[...], NT)
    narrow = dot(picked[:queries, :], low_ref[...], NT)
    total = (wide[:queries] + (wide[queries:] + narrow)).reshape(slices, group, tile)
    each = half // tile
    cols = pl.ds(pl.multiple_of(lax.rem(step, each) * tile, tile), tile)
    for h in range(sub // group):

        @pl.when(lax.div(step, each) == h)
        def _():
            out_ref[:, h * group : (h + 1) * group, cols] = total


def partial_scores(recv, order, high, low, slices, tile=256):
    queries, per, rank = recv.shape
    store, width = high.shape
    group = queries // slices
    sub = 8
    half = store * group // sub
    piece = pl.BlockSpec((tile, width), lambda n: (n, 0))
    return pl.pallas_call(
        scores_kernel,
        grid=(store // tile,),
        in_specs=[WHOLE, WHOLE, piece, piece],
        out_specs=WHOLE,
        out_shape=pltpu.VMEM((slices, sub, half), F32),
        scratch_shapes=[pltpu.VMEM((2 * queries, width), BF16)],
        compiler_params=limit(12),
        name="scores",
    )(near(recv), order.reshape(1, queries), far(high), far(low))


def sum_kernel(parts_ref, out_ref):
    total = jnp.sum(parts_ref[...], axis=0)
    group, store = out_ref.shape
    half = parts_ref.shape[2]
    for h in range(store // half):
        out_ref[:, h * half : (h + 1) * half] = total[h * group : (h + 1) * group]


def sum_parts(parts):
    slices, sub, half = parts.shape
    group = 4
    return pl.pallas_call(
        sum_kernel,
        in_specs=[WHOLE],
        out_specs=WHOLE,
        out_shape=jax.ShapeDtypeStruct((group, sub // group * half), F32),
        name="sum_parts",
    )(near(parts))


def per_device(rows, slices, activations, out_grads, proj_in, proj_out, inv_in, inv_out, stored, query_order):
    mine = preconditioned(activations, out_grads, proj_in, proj_out, inv_in, inv_out, rows, slices)
    mine = mine.reshape((rows * slices,) + mine.shape[2:])
    recv = lax.all_to_all(mine, ("row", "feat"), 0, 0, tiled=True)
    high, low = split_stored(stored)
    parts = partial_scores(recv, query_order, high, low, slices)
    return sum_parts(lax.all_to_all(parts, "feat", 0, 0, tiled=True))


def solution(mesh):
    placed = (
        P(None, ("row", "feat"), None),
        P(None, ("row", "feat"), None),
        P(),
        P(),
        P(),
        P(),
        P("row", None, "feat"),
        P(),
    )
    return jax.shard_map(
        functools.partial(per_device, mesh.shape["row"], mesh.shape["feat"]),
        mesh=mesh,
        in_specs=placed,
        out_specs=P("feat", "row"),
        check_vma=False,
    )
```

time: 758 us -> 114 us (0.15)
  waiting for transfers between devices: 704 us -> 0.01 us
  Pallas kernels: 0 us -> 73.3 us
  matrix products: 30 us -> 0 us
  blocking collectives: 0 us -> 27.6 us
  between operations: 14.2 us -> 0.03 us
  starting transfers between devices: 0.04 us -> 11.1 us
    unnamed x3 -> x0, waiting for transfers between devices: 353 us -> none
    all_gather x1 -> x0, waiting for transfers between devices: 351 us -> none  [per_device(): gathered = lax.all_gather(flat_grads, ('row', 'feat'), axis=0, tiled=True)]
    pallas_call x0 -> x4, Pallas kernels: none -> 73.3 us  [the longest x1 51.8 us: split_stored(): pl.pallas_call(split_kernel, grid=(store // block,), in_specs=[pl.BlockSp...]
    dot_general x6 -> x0, matrix products: 30 us -> none  [the longest x1 22.1 us: per_device(): jnp.einsum('qlf,slf->qs', picked, stored, precision=highest)]
    all_to_all x0 -> x1, blocking collectives: none -> 27.6 us  [per_device(): return sum_parts(lax.all_to_all(parts, 'feat', 0, 0, tiled=True))]
    all_to_all x0 -> x1, starting transfers between devices: none -> 11.1 us  [per_device(): recv = lax.all_to_all(mine, ('row', 'feat'), 0, 0, tiled=True)]
  transfers between devices with their start and end apart: 2 -> 1, of which waited for: 2 -> 0; matrix products, arithmetic and copies ran while one was open for 0% -> 0% of each run, Pallas kernels for 0% -> 45%
where the time goes in v1:
time: 114 us
  Pallas kernels  73.3 us (64%)
  blocking collectives  27.6 us (24%)
  starting transfers between devices  11.1 us (10%)
  local copies, waits for them, and re-layouts  1.91 us (2%)
    pallas_call x1, Pallas kernels, split_stored(): pl.pallas_call(split_kernel, grid=(store // block,), in_specs=[pl.BlockSp...  51.8 us
    all_to_all x1, blocking collectives, per_device(): return sum_parts(lax.all_to_all(parts, 'feat', 0, 0, tiled=True))  27.6 us
    pallas_call x1, Pallas kernels, partial_scores(): pl.pallas_call(scores_kernel, grid=(store // tile,), in_specs=[WHOLE, WHO...  13.4 us
    all_to_all x1, starting transfers between devices, per_device(): recv = lax.all_to_all(mine, ('row', 'feat'), 0, 0, tiled=True)  11.1 us
    pallas_call x1, Pallas kernels, preconditioned(): pl.pallas_call(precond_kernel, grid=(width // block,), in_specs=[tokens,...  7.47 us
  transfers between devices with their start and end apart: 1, of which 0 were waited for; matrix products, arithmetic and copies ran while one was open for 0% of the time, Pallas kernels for 45%

profile of v1, /device:TPU:0, one launch (start us, length us, event | category | flops | bytes accessed | tf_op | source)
XLA Modules:
  0.0 114.1 jit_solution(5385043657505067316)
XLA Ops:
  0.0 0.0 copy-start
  0.0 0.9 copy-done
  1.0 0.0 copy-start.1
  1.0 0.9 copy-done.1
  1.9 7.5 %precond.1 = f32[4,32,16,128]{3,2,1,0:T(8,128)} custom-call(f32[4,32,4096]{2,1,0:T(8,128)} %acts_ref.1, f32[4,32,4096]{2,1,0:T(8,128)} %grads_ref.1, f32[4096,128]{1,0:T(8,128)} %pin_ref.1, f32[4096,128]{1,0:T(8,128)} %pout_ref.1, f32[4,128,128]{2,1,0:T(8,128)S(1)} %copy-done, f32[4,128,128]{2,1,0:T(8,128)S(1)} %copy-done.1), custom_call_target="tpu_custom_call" | custom-call | tf_op jit(solution)/shard_map/precond/pallas_call | solution.py:86
  9.4 11.1 %all-to-all-start = ((f32[128,16,128]{2,1,0:T(8,128)}), f32[128,16,128]{2,1,0:T(8,128)S(1)}, u32[]{:S(2)}, u32[]{:S(2)}) async-start(f32[128,16,128]{2,1,0:T(8,128)} %bitcast), calls=%async_computation | async-start | bytes 2097152 | tf_op jit(solution)/shard_map/all_to_all | solution.py:191
  20.5 0.0 copy-start.2
  20.5 51.8 %split_stored.1 = (bf16[2048,2048]{1,0:T(8,128)(2,1)}, bf16[2048,2048]{1,0:T(8,128)(2,1)}) custom-call(f32[2048,4,512]{2,1,0:T(4,128)} %stored_ref.1), custom_call_target="tpu_custom_call" | custom-call | flops 33554432 | bytes 33554432 | tf_op jit(solution)/shard_map/split_stored/pallas_call | solution.py:108
  72.4 0.0 all-to-all-done.recv_ref
  72.4 0.0 copy-done.2
  72.4 13.4 %scores.1 = f32[32,8,1024]{2,1,0:T(8,128)S(1)} custom-call(f32[128,16,128]{2,1,0:T(8,128)S(1)} %all-to-all-done.recv_ref, s32[1,128]{1,0:T(1,128)S(1)} %bitcast.2, bf16[2048,2048]{1,0:T(8,128)(2,1)} %get-tuple-element.7.high_ref, bf16[2048,2048]{1,0:T(8,128)(2,1)} %get-tuple-element.8.low_ref), custom_call_target="tpu_custom_call" | custom-call | tf_op jit(solution)/shard_map/scores/pallas_call | solution.py:156
  85.7 27.6 %all_to_all.10.parts_ref = f32[32,8,1024]{2,1,0:T(8,128)S(1)} all-to-all(f32[32,8,1024]{2,1,0:T(8,128)S(1)} %scores.1), channel_id=1, replica_groups=mesh['row'=4,'feat'=32] {'feat'}, dimensions={0} | all-to-all | bytes 2097152 | tf_op jit(solution)/shard_map/all_to_all | solution.py:194
  113.4 0.7 sum_parts.1
Async XLA Ops:
  0.0 0.9 copy-start
  1.0 0.9 copy-start.1
  9.4 63.0 %all-to-all-start = ((f32[128,16,128]{2,1,0:T(8,128)}), f32[128,16,128]{2,1,0:T(8,128)S(1)}, u32[]{:S(2)}, u32[]{:S(2)}) async-start(f32[128,16,128]{2,1,0:T(8,128)} %bitcast), calls=%async_computation | async-start | bytes 2097152 | tf_op jit(solution)/shard_map/all_to_all | solution.py:191
  20.5 51.9 %copy-start.2 = (s32[128]{0:T(128)S(1)}, s32[128]{0:T(128)}, u32[]{:S(2)}) copy-start(s32[128]{0:T(128)} %param.15) | copy-start | bytes 1540

commit v2 on v1

v2 whole, which is shorter than its diff:
```python
import functools

import jax
import jax.numpy as jnp
from jax import lax
from jax.experimental import pallas as pl
from jax.experimental.pallas import tpu as pltpu
from jax.sharding import PartitionSpec as P

TOK = 32
F32, BF16 = jnp.float32, jnp.bfloat16
NN = (((1,), (0,)), ((), ()))
NT = (((1,), (1,)), ((), ()))
TN = (((0,), (0,)), ((), ()))
MIB = 1024 * 1024
WHOLE = pl.BlockSpec(memory_space=pltpu.VMEM)
ANYWHERE = pl.BlockSpec(memory_space=pl.ANY)


def limit(mib):
    return pltpu.CompilerParams(vmem_limit_bytes=mib * MIB)


def near(x):
    return pltpu.with_memory_space_constraint(x, pltpu.VMEM)


def far(x):
    return pltpu.with_memory_space_constraint(x, pltpu.HBM)


def dot(a, b, dims=NN):
    return lax.dot_general(a, b, dims, preferred_element_type=F32)


def pieces(x):
    high = x.astype(BF16)
    return high, (x - high.astype(F32)).astype(BF16)


def wide_product(x, w, flip=False):
    rows, cols = x.shape[0], w.shape[0 if flip else 1]
    left, right = jnp.concatenate(pieces(x), axis=0), jnp.concatenate(pieces(w), axis=0 if flip else 1)
    both = dot(left, right, NT if flip else NN)
    return (both[rows:, cols:] + both[rows:, :cols]) + both[:rows, cols:] + both[:rows, :cols]


def precond_kernel(acts_hbm, pin_hbm, grads_hbm, pout_hbm, iin_hbm, iout_hbm, out_ref, acts, pin, grads, pout, iin, iout, sems):
    layers, tok, width = acts.shape
    rank = pin.shape[1]
    count = sems.shape[1]
    chunk = width // count

    def copies(i):
        at = pl.ds(i * chunk, chunk)
        return [
            pltpu.make_async_copy(acts_hbm.at[:, :, at], acts.at[:, :, at], sems.at[0, i]),
            pltpu.make_async_copy(pin_hbm.at[at, :], pin.at[at, :], sems.at[1, i]),
            pltpu.make_async_copy(grads_hbm.at[:, :, at], grads.at[:, :, at], sems.at[2, i]),
            pltpu.make_async_copy(pout_hbm.at[at, :], pout.at[at, :], sems.at[3, i]),
        ]

    factors = [
        pltpu.make_async_copy(iin_hbm, iin, sems.at[4, 0]),
        pltpu.make_async_copy(iout_hbm, iout, sems.at[4, 1]),
    ]
    for i in range(count):
        for copy in copies(i):
            copy.start()
    for copy in factors:
        copy.start()
    acts_low = grads_low = jnp.zeros((layers * tok, rank), F32)
    for i in range(count):
        for copy in copies(i):
            copy.wait()
        at = slice(i * chunk, (i + 1) * chunk)
        acts_low += wide_product(acts[:, :, at].reshape(layers * tok, chunk), pin[at, :])
        grads_low += wide_product(grads[:, :, at].reshape(layers * tok, chunk), pout[at, :])
    for copy in factors:
        copy.wait()
    rows, slices, per, _ = out_ref.shape
    per = per // layers
    for l in range(layers):
        mine = slice(l * tok, (l + 1) * tok)
        right = wide_product(acts_low[mine, :], iin[l])
        left = wide_product(grads_low[mine, :], iout[l], flip=True)
        (left_high, left_low), (right_high, right_low) = pieces(left), pieces(right)
        tall = jnp.concatenate([left_low, left_low, left_high, left_high], axis=0)
        other = jnp.concatenate([right_low, right_high, right_low, right_high], axis=0)
        cond = dot(tall, other, TN).reshape(slices, per, rank)
        for r in range(rows):
            out_ref[r, :, l * per : (l + 1) * per, :] = cond


def preconditioned(activations, out_grads, proj_in, proj_out, inv_in, inv_out, rows, slices, count=4):
    layers, tok, width = activations.shape
    rank = proj_in.shape[1]
    tokens = pltpu.VMEM((layers, tok, width), F32)
    side = pltpu.VMEM((width, rank), F32)
    factor = pltpu.VMEM((layers, rank, rank), F32)
    return pl.pallas_call(
        precond_kernel,
        in_specs=[ANYWHERE] * 6,
        out_specs=WHOLE,
        out_shape=pltpu.VMEM((rows, slices, layers * (rank // slices), rank), F32),
        scratch_shapes=[tokens, side, tokens, side, factor, factor, pltpu.SemaphoreType.DMA((5, count))],
        compiler_params=limit(24),
        name="precond",
    )(far(activations), far(proj_in), far(out_grads), far(proj_out), far(inv_in), far(inv_out))


def tiles_view(stored, lanes=128):
    store, layers, width = stored.shape
    runs = width // lanes
    return stored.reshape(store, layers, runs, lanes).transpose(0, 2, 1, 3).reshape(store, runs * layers, lanes)


def split_kernel(layers, tiles_hbm, high_ref, low_ref, rows, sems):
    step = pl.program_id(0)
    _, per, lanes = tiles_hbm.shape
    place = [(t % layers) * (per // layers) + t // layers for t in range(per)]
    block = rows.shape[1]

    def copies(s, slot):
        at = pl.ds(pl.multiple_of(s * block, block), block)
        return [
            pltpu.make_async_copy(tiles_hbm.at[at, t, :], rows.at[slot, :, pl.ds(place[t] * lanes, lanes)], sems.at[slot, t])
            for t in range(per)
        ]

    @pl.when(step == 0)
    def _():
        for copy in copies(0, 0):
            copy.start()

    @pl.when(step + 1 < pl.num_programs(0))
    def _():
        for copy in copies(step + 1, lax.rem(step + 1, 2)):
            copy.start()

    slot = lax.rem(step, 2)
    for copy in copies(step, slot):
        copy.wait()
    high_ref[...], low_ref[...] = pieces(rows[slot])


def split_stored(stored, block=256):
    tiles = tiles_view(stored)
    store, per, lanes = tiles.shape
    half = pl.BlockSpec((block, per * lanes), lambda s: (s, 0))
    return pl.pallas_call(
        functools.partial(split_kernel, stored.shape[1]),
        grid=(store // block,),
        in_specs=[ANYWHERE],
        out_specs=[half, half],
        out_shape=[pltpu.HBM((store, per * lanes), BF16)] * 2,
        scratch_shapes=[pltpu.VMEM((2, block, per * lanes), F32), pltpu.SemaphoreType.DMA((2, per))],
        compiler_params=limit(24),
        cost_estimate=pl.CostEstimate(flops=stored.size * 8, bytes_accessed=stored.size * 8, transcendentals=0),
        name="split_stored",
    )(far(tiles))


def scores_kernel(recv_ref, order_ref, high_hbm, low_hbm, out_ref, high, low, rows, picked, row_sems, sems):
    queries, per, rank = recv_ref.shape
    slices, sub, half = out_ref.shape
    group = queries // slices
    store = high.shape[0]
    count = sems.shape[1]
    chunk = store // count
    tile = 256

    def copies(i):
        at = pl.ds(i * chunk, chunk)
        return [
            pltpu.make_async_copy(high_hbm.at[at, :], high.at[at, :], sems.at[0, i]),
            pltpu.make_async_copy(low_hbm.at[at, :], low.at[at, :], sems.at[1, i]),
        ]

    lined = [
        pltpu.make_async_copy(recv_ref.at[:, t, :], rows.at[:, pl.ds(t * rank, rank)], row_sems.at[t])
        for t in range(per)
    ]
    for copy in lined:
        copy.start()
    for i in range(count):
        for copy in copies(i):
            copy.start()
    ids = lax.broadcasted_iota(jnp.int32, (queries, queries), 0)
    chosen = (ids == order_ref[...]).astype(F32).astype(BF16)
    for copy in lined:
        copy.wait()
    rows_high, rows_low = pieces(rows[...])
    picked[:queries, :] = dot(chosen, rows_high, TN).astype(BF16)
    picked[queries:, :] = dot(chosen, rows_low, TN).astype(BF16)
    for n in range(store // tile):
        if n * tile % chunk == 0:
            for copy in copies(n * tile // chunk):
                copy.wait()
        at = slice(n * tile, (n + 1) * tile)
        wide = dot(high[at, :], picked[...], NT)
        narrow = dot(low[at, :], picked[:queries, :], NT)
        total = (wide[:, :queries] + (wide[:, queries:] + narrow)).T
        h, c = divmod(n * tile, half)
        out_ref[:, h * group : (h + 1) * group, c : c + tile] = total.reshape(slices, group, tile)


def partial_scores(recv, order, high, low, slices, count=4):
    queries, per, rank = recv.shape
    store, width = high.shape
    sub = 8
    half = store * (queries // slices) // sub
    return pl.pallas_call(
        scores_kernel,
        in_specs=[WHOLE, WHOLE, ANYWHERE, ANYWHERE],
        out_specs=WHOLE,
        out_shape=pltpu.VMEM((slices, sub, half), F32),
        scratch_shapes=[
            pltpu.VMEM((store, width), BF16),
            pltpu.VMEM((store, width), BF16),
            pltpu.VMEM((queries, width), F32),
            pltpu.VMEM((2 * queries, width), BF16),
            pltpu.SemaphoreType.DMA((per,)),
            pltpu.SemaphoreType.DMA((2, count)),
        ],
        compiler_params=limit(32),
        name="scores",
    )(near(recv), order.reshape(1, queries), far(high), far(low))


def sum_kernel(parts_ref, out_ref):
    total = jnp.sum(parts_ref[...], axis=0)
    group, store = out_ref.shape
    half = parts_ref.shape[2]
    for h in range(store // half):
        out_ref[:, h * half : (h + 1) * half] = total[h * group : (h + 1) * group]


def sum_parts(parts):
    slices, sub, half = parts.shape
    group = 4
    return pl.pallas_call(
        sum_kernel,
        in_specs=[WHOLE],
        out_specs=WHOLE,
        out_shape=jax.ShapeDtypeStruct((group, sub // group * half), F32),
        name="sum_parts",
    )(near(parts))


def per_device(rows, slices, activations, out_grads, proj_in, proj_out, inv_in, inv_out, stored, query_order):
    mine = preconditioned(activations, out_grads, proj_in, proj_out, inv_in, inv_out, rows, slices)
    mine = mine.reshape((rows * slices,) + mine.shape[2:])
    recv = lax.all_to_all(mine, ("row", "feat"), 0, 0, tiled=True)
    high, low = split_stored(stored)
    parts = partial_scores(recv, query_order, high, low, slices)
    return sum_parts(lax.all_to_all(parts, "feat", 0, 0, tiled=True))


def solution(mesh):
    placed = (
        P(None, ("row", "feat"), None),
        P(None, ("row", "feat"), None),
        P(),
        P(),
        P(),
        P(),
        P("row", None, "feat"),
        P(),
    )
    return jax.shard_map(
        functools.partial(per_device, mesh.shape["row"], mesh.shape["feat"]),
        mesh=mesh,
        in_specs=placed,
        out_specs=P("feat", "row"),
        check_vma=False,
    )
```

time: 114 us -> 69.4 us (0.61)
  Pallas kernels: 73.3 us -> 30.2 us
  waiting for transfers between devices: 0.01 us -> 2.84 us
  blocking collectives: 27.6 us -> 24.9 us
  local copies, waits for them, and re-layouts: 1.91 us -> 0.01 us
    pallas_call x3, Pallas kernels: 72.7 us -> 29.5 us  [the longest x1 15.1 us: split_stored(): pl.pallas_call(functools.partial(split_kernel, stored.shape[1]), grid=(st...]
    all_to_all x1, waiting for transfers between devices: 0.01 us -> 2.84 us  [per_device(): recv = lax.all_to_all(mine, ('row', 'feat'), 0, 0, tiled=True)]
    all_to_all x1, blocking collectives: 27.6 us -> 24.9 us  [per_device(): return sum_parts(lax.all_to_all(parts, 'feat', 0, 0, tiled=True))]
    unnamed x6 -> x2, local copies, waits for them, and re-layouts: 1.91 us -> 0.01 us
  transfers between devices with their start and end apart: 1 -> 1, of which waited for: 0 -> 1; matrix products, arithmetic and copies ran while one was open for 0% -> 0% of each run, Pallas kernels for 45% -> 22%
where the time goes in v2:
time: 69.4 us; the launch traced here: 69.1 us
  Pallas kernels  30.2 us (44%)
  blocking collectives  24.9 us (36%)
  starting transfers between devices  11.1 us (16%)
  waiting for transfers between devices  2.84 us (4%)
    all_to_all x1, blocking collectives, per_device(): return sum_parts(lax.all_to_all(parts, 'feat', 0, 0, tiled=True))  24.9 us
    pallas_call x1, Pallas kernels, split_stored(): pl.pallas_call(functools.partial(split_kernel, stored.shape[1]), grid=(st...  15.1 us
    all_to_all x1, starting transfers between devices, per_device(): recv = lax.all_to_all(mine, ('row', 'feat'), 0, 0, tiled=True)  11.1 us
    pallas_call x1, Pallas kernels, partial_scores(): pl.pallas_call(scores_kernel, in_specs=[WHOLE, WHOLE, ANYWHERE, ANYWHERE]...  8.52 us
    pallas_call x1, Pallas kernels, preconditioned(): pl.pallas_call(precond_kernel, in_specs=[ANYWHERE] * 6, out_specs=WHOLE,...  5.94 us
    all_to_all x1, waiting for transfers between devices, per_device(): recv = lax.all_to_all(mine, ('row', 'feat'), 0, 0, tiled=True)  2.84 us
  transfers between devices with their start and end apart: 1, of which 1 were waited for; matrix products, arithmetic and copies ran while one was open for 0% of the time, Pallas kernels for 22%

profile of v2, /device:TPU:0, one launch (start us, length us, event | category | flops | bytes accessed | tf_op | source)
XLA Modules:
  0.0 69.1 jit_solution(3920299230353608189)
XLA Ops:
  0.0 5.9 %precond.1 = f32[4,32,16,128]{3,2,1,0:T(8,128)} custom-call(f32[4,32,4096]{2,1,0:T(8,128)} %acts_hbm.1, f32[4096,128]{1,0:T(8,128)} %pin_hbm.1, f32[4,32,4096]{2,1,0:T(8,128)} %grads_hbm.1, f32[4096,128]{1,0:T(8,128)} %pout_hbm.1, f32[4,128,128]{2,1,0:T(8,128)} %iin_hbm.1, f32[4,128,128]{2,1,0:T(8,128)} %iout_hbm.1), custom_call_target="tpu_custom_call" | custom-call | tf_op jit(solution)/shard_map/precond/pallas_call | solution.py:101
  5.9 11.1 %all-to-all-start = ((f32[128,16,128]{2,1,0:T(8,128)}), f32[128,16,128]{2,1,0:T(8,128)S(1)}, u32[]{:S(2)}, u32[]{:S(2)}) async-start(f32[128,16,128]{2,1,0:T(8,128)} %bitcast), calls=%async_computation | async-start | bytes 2097152 | tf_op jit(solution)/shard_map/all_to_all | solution.py:254
  17.1 0.0 copy-start
  17.1 15.1 %split_stored.1 = (bf16[2048,2048]{1,0:T(8,128)(2,1)}, bf16[2048,2048]{1,0:T(8,128)(2,1)}) custom-call(f32[2048,16,128]{2,1,0:T(8,128)} %bitcast.8), custom_call_target="tpu_custom_call" | custom-call | flops 33554432 | bytes 33554432 | tf_op jit(solution)/shard_map/split_stored/pallas_call | solution.py:151
  32.2 2.8 %all-to-all-done.recv_ref = f32[128,16,128]{2,1,0:T(8,128)S(1)} async-done(((f32[128,16,128]{2,1,0:T(8,128)}), f32[128,16,128]{2,1,0:T(8,128)S(1)}, u32[]{:S(2)}, u32[]{:S(2)}) %all-to-all-start) | async-done | bytes 1048608 | tf_op jit(solution)/shard_map/all_to_all | solution.py:254
  35.0 0.0 copy-done
  35.0 8.5 %scores.1 = f32[32,8,1024]{2,1,0:T(8,128)S(1)} custom-call(f32[128,16,128]{2,1,0:T(8,128)S(1)} %all-to-all-done.recv_ref, s32[1,128]{1,0:T(1,128)S(1)} %bitcast.7, bf16[2048,2048]{1,0:T(8,128)(2,1)} %get-tuple-element.7.high_hbm, bf16[2048,2048]{1,0:T(8,128)(2,1)} %get-tuple-element.8.low_hbm), custom_call_target="tpu_custom_call" | custom-call | tf_op jit(solution)/shard_map/scores/pallas_call | solution.py:213
  43.6 24.9 %all_to_all.10.parts_ref = f32[32,8,1024]{2,1,0:T(8,128)S(1)} all-to-all(f32[32,8,1024]{2,1,0:T(8,128)S(1)} %scores.1), channel_id=1, replica_groups=mesh['row'=4,'feat'=32] {'feat'}, dimensions={0} | all-to-all | bytes 2097152 | tf_op jit(solution)/shard_map/all_to_all | solution.py:257
  68.4 0.7 sum_parts.1
Async XLA Ops:
  5.9 29.1 %all-to-all-start = ((f32[128,16,128]{2,1,0:T(8,128)}), f32[128,16,128]{2,1,0:T(8,128)S(1)}, u32[]{:S(2)}, u32[]{:S(2)}) async-start(f32[128,16,128]{2,1,0:T(8,128)} %bitcast), calls=%async_computation | async-start | bytes 2097152 | tf_op jit(solution)/shard_map/all_to_all | solution.py:254
  17.1 17.9 %copy-start = (s32[128]{0:T(128)S(1)}, s32[128]{0:T(128)}, u32[]{:S(2)}) copy-start(s32[128]{0:T(128)} %param.15) | copy-start | bytes 1540

commit v3 on v2

v3 whole, which is shorter than its diff:
```python
import functools

import jax
import jax.numpy as jnp
from jax import lax
from jax.experimental import pallas as pl
from jax.experimental.pallas import tpu as pltpu
from jax.sharding import PartitionSpec as P

TOK = 32
F32, BF16 = jnp.float32, jnp.bfloat16
NN = (((1,), (0,)), ((), ()))
NT = (((1,), (1,)), ((), ()))
TN = (((0,), (0,)), ((), ()))
MIB = 1024 * 1024
WHOLE = pl.BlockSpec(memory_space=pltpu.VMEM)
ANYWHERE = pl.BlockSpec(memory_space=pl.ANY)


def limit(mib):
    return pltpu.CompilerParams(vmem_limit_bytes=mib * MIB)


def near(x):
    return pltpu.with_memory_space_constraint(x, pltpu.VMEM)


def far(x):
    return pltpu.with_memory_space_constraint(x, pltpu.HBM)


def dot(a, b, dims=NN):
    return lax.dot_general(a, b, dims, preferred_element_type=F32)


def pieces(x):
    high = x.astype(BF16)
    return high, (x - high.astype(F32)).astype(BF16)


def wide_product(x, w, flip=False):
    rows, cols = x.shape[0], w.shape[0 if flip else 1]
    left, right = jnp.concatenate(pieces(x), axis=0), jnp.concatenate(pieces(w), axis=0 if flip else 1)
    both = dot(left, right, NT if flip else NN)
    return (both[rows:, cols:] + both[rows:, :cols]) + both[:rows, cols:] + both[:rows, :cols]


def project_kernel(acts_hbm, pin_hbm, grads_hbm, pout_hbm, acts_low_ref, grads_low_ref, acts, pin, grads, pout, sems):
    layers, tok, width = acts.shape
    rank = pin.shape[1]
    count = sems.shape[1]
    chunk = width // count

    def copies(i):
        at = pl.ds(i * chunk, chunk)
        return [
            pltpu.make_async_copy(acts_hbm.at[:, :, at], acts.at[:, :, at], sems.at[0, i]),
            pltpu.make_async_copy(pin_hbm.at[at, :], pin.at[at, :], sems.at[1, i]),
            pltpu.make_async_copy(grads_hbm.at[:, :, at], grads.at[:, :, at], sems.at[2, i]),
            pltpu.make_async_copy(pout_hbm.at[at, :], pout.at[at, :], sems.at[3, i]),
        ]

    for i in range(count):
        for copy in copies(i):
            copy.start()
    acts_low = grads_low = jnp.zeros((layers * tok, rank), F32)
    for i in range(count):
        for copy in copies(i):
            copy.wait()
        at = slice(i * chunk, (i + 1) * chunk)
        acts_low += wide_product(acts[:, :, at].reshape(layers * tok, chunk), pin[at, :])
        grads_low += wide_product(grads[:, :, at].reshape(layers * tok, chunk), pout[at, :])
    acts_low_ref[...] = acts_low
    grads_low_ref[...] = grads_low


def projected(activations, out_grads, proj_in, proj_out, count=4):
    layers, tok, width = activations.shape
    rank = proj_in.shape[1]
    tokens = pltpu.VMEM((layers, tok, width), F32)
    side = pltpu.VMEM((width, rank), F32)
    return pl.pallas_call(
        project_kernel,
        in_specs=[ANYWHERE] * 4,
        out_specs=[WHOLE] * 2,
        out_shape=[pltpu.VMEM((layers * tok, rank), F32)] * 2,
        scratch_shapes=[tokens, side, tokens, side, pltpu.SemaphoreType.DMA((4, count))],
        compiler_params=limit(12),
        name="projected",
    )(far(activations), far(proj_in), far(out_grads), far(proj_out))


def precond_kernel(acts_low, grads_low, iin, iout, out_ref):
    rows, slices, per, rank = out_ref.shape
    layers = iin.shape[0]
    tok = acts_low.shape[0] // layers
    per = per // layers
    for l in range(layers):
        mine = slice(l * tok, (l + 1) * tok)
        right = wide_product(acts_low[mine, :], iin[l])
        left = wide_product(grads_low[mine, :], iout[l], flip=True)
        (left_high, left_low), (right_high, right_low) = pieces(left), pieces(right)
        tall = jnp.concatenate([left_low, left_low, left_high, left_high], axis=0)
        other = jnp.concatenate([right_low, right_high, right_low, right_high], axis=0)
        cond = dot(tall, other, TN).reshape(slices, per, rank)
        for r in range(rows):
            out_ref[r, :, l * per : (l + 1) * per, :] = cond


def preconditioned(acts_low, grads_low, inv_in, inv_out, rows, slices):
    layers, rank, _ = inv_in.shape
    return pl.pallas_call(
        precond_kernel,
        in_specs=[WHOLE] * 4,
        out_specs=WHOLE,
        out_shape=pltpu.VMEM((rows, slices, layers * (rank // slices), rank), F32),
        compiler_params=limit(4),
        cost_estimate=pl.CostEstimate(flops=1 << 33, bytes_accessed=1 << 20, transcendentals=0),
        name="precond",
    )(near(acts_low), near(grads_low), near(inv_in), near(inv_out))


def tiles_view(stored, lanes=128):
    store, layers, width = stored.shape
    runs = width // lanes
    return stored.reshape(store, layers, runs, lanes).transpose(0, 2, 1, 3).reshape(store, runs * layers, lanes)


def scores_kernel(layers, recv_ref, order_ref, tiles_ref, out_ref, rows, picked, sems):
    queries, per, rank = recv_ref.shape
    slices, sub, half = out_ref.shape
    group = queries // slices
    store = tiles_ref.shape[0]
    runs = per // layers
    tile = 256
    lined = []
    for t in range(per):
        place = (t % runs) * layers + t // runs
        lined.append(pltpu.make_async_copy(recv_ref.at[:, t, :], rows.at[:, pl.ds(place * rank, rank)], sems.at[t]))
    for copy in lined:
        copy.start()
    ids = lax.broadcasted_iota(jnp.int32, (queries, queries), 0)
    chosen = (ids == order_ref[...]).astype(F32).astype(BF16)
    for copy in lined:
        copy.wait()
    rows_high, rows_low = pieces(rows[...])
    picked[:queries, :] = dot(chosen, rows_high, TN).astype(BF16)
    picked[queries:, :] = dot(chosen, rows_low, TN).astype(BF16)
    for n in range(store // tile):
        high, low = pieces(tiles_ref[n * tile : (n + 1) * tile].reshape(tile, per * rank))
        wide = dot(high, picked[...], NT)
        narrow = dot(low, picked[:queries, :], NT)
        total = (wide[:, :queries] + (wide[:, queries:] + narrow)).T
        h, c = divmod(n * tile, half)
        out_ref[:, h * group : (h + 1) * group, c : c + tile] = total.reshape(slices, group, tile)


def partial_scores(recv, order, stored, slices):
    queries, per, rank = recv.shape
    store, layers, _ = stored.shape
    sub = 8
    half = store * (queries // slices) // sub
    return pl.pallas_call(
        functools.partial(scores_kernel, layers),
        in_specs=[WHOLE] * 3,
        out_specs=WHOLE,
        out_shape=pltpu.VMEM((slices, sub, half), F32),
        scratch_shapes=[
            pltpu.VMEM((queries, per * rank), F32),
            pltpu.VMEM((2 * queries, per * rank), BF16),
            pltpu.SemaphoreType.DMA((per,)),
        ],
        compiler_params=limit(4),
        name="scores",
    )(near(recv), order.reshape(1, queries), near(tiles_view(stored)))


def sum_kernel(parts_ref, out_ref):
    total = jnp.sum(parts_ref[...], axis=0)
    group, store = out_ref.shape
    half = parts_ref.shape[2]
    for h in range(store // half):
        out_ref[:, h * half : (h + 1) * half] = total[h * group : (h + 1) * group]


def sum_parts(parts):
    slices, sub, half = parts.shape
    group = 4
    return pl.pallas_call(
        sum_kernel,
        in_specs=[WHOLE],
        out_specs=WHOLE,
        out_shape=jax.ShapeDtypeStruct((group, sub // group * half), F32),
        name="sum_parts",
    )(near(parts))


def per_device(rows, slices, activations, out_grads, proj_in, proj_out, inv_in, inv_out, stored, query_order):
    acts_low, grads_low = projected(activations, out_grads, proj_in, proj_out)
    mine = preconditioned(acts_low, grads_low, inv_in, inv_out, rows, slices)
    mine = mine.reshape((rows * slices,) + mine.shape[2:])
    recv = lax.all_to_all(mine, ("row", "feat"), 0, 0, tiled=True)
    parts = partial_scores(recv, query_order, stored, slices)
    return sum_parts(lax.all_to_all(parts, "feat", 0, 0, tiled=True))


def solution(mesh):
    placed = (
        P(None, ("row", "feat"), None),
        P(None, ("row", "feat"), None),
        P(),
        P(),
        P(),
        P(),
        P("row", None, "feat"),
        P(),
    )
    return jax.shard_map(
        functools.partial(per_device, mesh.shape["row"], mesh.shape["feat"]),
        mesh=mesh,
        in_specs=placed,
        out_specs=P("feat", "row"),
        check_vma=False,
    )
```

time: 69.4 us -> 64.3 us (0.927)
  blocking collectives: 24.9 us -> 51.9 us
  Pallas kernels: 30.2 us -> 12.2 us
  starting transfers between devices: 11.1 us -> 0 us
  waiting for transfers between devices: 2.84 us -> 0 us
    all_to_all x0 -> x1, blocking collectives: none -> 28.9 us  [per_device(): recv = lax.all_to_all(mine, ('row', 'feat'), 0, 0, tiled=True)]
    pallas_call x3, Pallas kernels: 29.5 us -> 11.5 us  [the longest x1 6.57 us: partial_scores(): pl.pallas_call(functools.partial(scores_kernel, layers), in_specs=[WHOLE]...]
    all_to_all x1 -> x0, starting transfers between devices: 11.1 us -> none  [per_device(): recv = lax.all_to_all(mine, ('row', 'feat'), 0, 0, tiled=True)]
    all_to_all x1 -> x0, waiting for transfers between devices: 2.84 us -> none  [per_device(): recv = lax.all_to_all(mine, ('row', 'feat'), 0, 0, tiled=True)]
    all_to_all x1, blocking collectives: 24.9 us -> 23 us  [per_device(): return sum_parts(lax.all_to_all(parts, 'feat', 0, 0, tiled=True))]
  transfers between devices with their start and end apart: 1 -> 0, of which waited for: 1 -> 0; matrix products, arithmetic and copies ran while one was open for 0% -> 0% of each run, Pallas kernels for 22% -> 0%
where the time goes in v3:
time: 64.3 us; the launch traced here: 64.2 us
  blocking collectives  51.9 us (81%)
  Pallas kernels  12.2 us (19%)
    all_to_all x1, blocking collectives, per_device(): recv = lax.all_to_all(mine, ('row', 'feat'), 0, 0, tiled=True)  28.9 us
    all_to_all x1, blocking collectives, per_device(): return sum_parts(lax.all_to_all(parts, 'feat', 0, 0, tiled=True))  23 us
    pallas_call x1, Pallas kernels, partial_scores(): pl.pallas_call(functools.partial(scores_kernel, layers), in_specs=[WHOLE]...  6.57 us
    pallas_call x1, Pallas kernels, projected(): pl.pallas_call(project_kernel, in_specs=[ANYWHERE] * 4, out_specs=[WHOLE]...  4.02 us

profile of v3, /device:TPU:0, one launch (start us, length us, event | category | flops | bytes accessed | tf_op | source)
XLA Modules:
  0.0 64.2 jit_solution(12351765092033213742)
XLA Ops:
  0.0 0.0 copy-start.2
  0.0 0.0 copy-start.1
  0.0 4.0 %projected.1 = (f32[128,128]{1,0:T(8,128)S(1)}, f32[128,128]{1,0:T(8,128)S(1)}) custom-call(f32[4,32,4096]{2,1,0:T(8,128)} %acts_hbm.1, f32[4096,128]{1,0:T(8,128)} %pin_hbm.1, f32[4,32,4096]{2,1,0:T(8,128)} %grads_hbm.1, f32[4096,128]{1,0:T(8,128)} %pout_hbm.1), custom_call_target="tpu_custom_call" | custom-call | tf_op jit(solution)/shard_map/projected/pallas_call | solution.py:82
  4.0 0.0 slice-start
  4.0 0.0 copy-done.2
  4.1 0.0 copy-done.1
  4.1 0.0 slice-start.1
  4.1 0.0 slice-start.2
  4.1 0.0 slice-start.3
  4.1 0.9 %precond.1 = f32[4,32,16,128]{3,2,1,0:T(8,128)S(1)} custom-call(f32[128,128]{1,0:T(8,128)S(1)} %get-tuple-element.7.acts_low, f32[128,128]{1,0:T(8,128)S(1)} %get-tuple-element.8.grads_low, f32[4,128,128]{2,1,0:T(8,128)S(1)} %copy-done.1, f32[4,128,128]{2,1,0:T(8,128)S(1)} %copy-done.2), custom_call_target="tpu_custom_call" | custom-call | flops 8589934592 | bytes 1048576 | tf_op jit(solution)/shard_map/precond/pallas_call | solution.py:112
  5.0 0.0 copy-start
  5.0 28.9 %all_to_all.10.recv_ref = f32[128,16,128]{2,1,0:T(8,128)S(1)} all-to-all(f32[128,16,128]{2,1,0:T(8,128)S(1)} %bitcast.10), channel_id=1, replica_groups=mesh['row'=4,'feat'=32] {'row','feat'}, dimensions={0} | all-to-all | bytes 2097152 | tf_op jit(solution)/shard_map/all_to_all | solution.py:202
  33.9 0.0 slice-done
  33.9 0.0 slice-done.1
  33.9 0.0 slice-done.2
  33.9 0.0 slice-done.3
  33.9 0.0 copy-done
  34.0 6.6 %scores.1 = f32[32,8,1024]{2,1,0:T(8,128)S(1)} custom-call(f32[128,16,128]{2,1,0:T(8,128)S(1)} %all_to_all.10.recv_ref, s32[1,128]{1,0:T(1,128)S(1)} %bitcast.11, f32[2048,16,128]{2,1,0:T(8,128)S(1)} %bitcast.9), custom_call_target="tpu_custom_call" | custom-call | tf_op jit(solution)/shard_map/scores/pallas_call | solution.py:163
  40.5 23.0 %all_to_all.11.parts_ref = f32[32,8,1024]{2,1,0:T(8,128)S(1)} all-to-all(f32[32,8,1024]{2,1,0:T(8,128)S(1)} %scores.1), channel_id=1, replica_groups=mesh['row'=4,'feat'=32] {'feat'}, dimensions={0} | all-to-all | bytes 2097152 | tf_op jit(solution)/shard_map/all_to_all | solution.py:204
  63.5 0.7 %sum_parts.1 = f32[4,2048]{1,0:T(4,128)} custom-call(f32[32,8,1024]{2,1,0:T(8,128)S(1)} %all_to_all.11.parts_ref), custom_call_target="tpu_custom_call" | custom-call | tf_op jit(solution)/shard_map/sum_parts/pallas_call | solution.py:189
  (1 shorter events, 0.0 us)
Async XLA Ops:
  0.0 4.0 %copy-start.2 = (f32[4,128,128]{2,1,0:T(8,128)S(1)}, f32[4,128,128]{2,1,0:T(8,128)}, u32[]{:S(2)}) copy-start(f32[4,128,128]{2,1,0:T(8,128)} %iout.1) | copy-start | bytes 786436
  0.0 4.1 %copy-start.1 = (f32[4,128,128]{2,1,0:T(8,128)S(1)}, f32[4,128,128]{2,1,0:T(8,128)}, u32[]{:S(2)}) copy-start(f32[4,128,128]{2,1,0:T(8,128)} %iin.1) | copy-start | bytes 786436
  4.0 29.9 %slice-start = ((s8[16777216]{0:T(1024)(128)(4,1)}), s8[4194304]{0:T(1024)(128)(4,1)S(1)}, s32[]{:S(2)}) async-start(s8[16777216]{0:T(1024)(128)(4,1)} %bitcast.7), calls=%async_computation.2 | async-start | bytes 8388608
  4.1 29.9 %slice-start.1 = ((s8[16777216]{0:T(1024)(128)(4,1)}), s8[4194304]{0:T(1024)(128)(4,1)S(1)}, s32[]{:S(2)}) async-start(s8[16777216]{0:T(1024)(128)(4,1)} %bitcast.7), calls=%async_computation.3 | async-start | bytes 8388608
  4.1 29.9 %slice-start.2 = ((s8[16777216]{0:T(1024)(128)(4,1)}), s8[4194304]{0:T(1024)(128)(4,1)S(1)}, s32[]{:S(2)}) async-start(s8[16777216]{0:T(1024)(128)(4,1)} %bitcast.7), calls=%async_computation.4 | async-start | bytes 8388608
  4.1 29.8 %slice-start.3 = ((s8[16777216]{0:T(1024)(128)(4,1)}), s8[4194304]{0:T(1024)(128)(4,1)S(1)}, s32[]{:S(2)}) async-start(s8[16777216]{0:T(1024)(128)(4,1)} %bitcast.7), calls=%async_computation.5 | async-start | bytes 8388608
  5.0 28.9 %copy-start = (s32[128]{0:T(128)S(1)}, s32[128]{0:T(128)}, u32[]{:S(2)}) copy-start(s32[128]{0:T(128)} %param.15) | copy-start | bytes 1540

commit v4 on v3

--- a/solution.py
+++ b/solution.py
@@ -7,7 +7,7 @@
 from jax.experimental.pallas import tpu as pltpu
 from jax.sharding import PartitionSpec as P
 
-TOK = 32
+ROWS, CORES = 4, 2
 F32, BF16 = jnp.float32, jnp.bfloat16
 NN = (((1,), (0,)), ((), ()))
 NT = (((1,), (1,)), ((), ()))
@@ -126,8 +126,17 @@
     return stored.reshape(store, layers, runs, lanes).transpose(0, 2, 1, 3).reshape(store, runs * layers, lanes)
 
 
-def scores_kernel(layers, recv_ref, order_ref, tiles_ref, out_ref, rows, picked, sems):
-    queries, per, rank = recv_ref.shape
+def positions(order, slices, mine):
+    bits = slices.bit_length() - 1
+    row = lax.shift_right_logical(order, bits)
+    other = jnp.where((row & (CORES - 1)) == mine, 0, 1)
+    pairs = ROWS // CORES
+    return (other * pairs + lax.shift_right_logical(row, CORES.bit_length() - 1)) * slices + (order & (slices - 1))
+
+
+def scores_kernel(layers, recv_ref, swapped_ref, order_ref, tiles_ref, out_ref, rows, picked, sems):
+    held, per, rank = recv_ref.shape
+    queries = CORES * held
     slices, sub, half = out_ref.shape
     group = queries // slices
     store = tiles_ref.shape[0]
@@ -136,11 +145,14 @@
     lined = []
     for t in range(per):
         place = (t % runs) * layers + t // runs
-        lined.append(pltpu.make_async_copy(recv_ref.at[:, t, :], rows.at[:, pl.ds(place * rank, rank)], sems.at[t]))
+        for c, part in enumerate((recv_ref, swapped_ref)):
+            to = rows.at[pl.ds(c * held, held), pl.ds(place * rank, rank)]
+            lined.append(pltpu.make_async_copy(part.at[:, t, :], to, sems.at[c, t]))
     for copy in lined:
         copy.start()
     ids = lax.broadcasted_iota(jnp.int32, (queries, queries), 0)
-    chosen = (ids == order_ref[...]).astype(F32).astype(BF16)
+    at = positions(order_ref[...], slices, lax.rem(lax.axis_index("row"), CORES))
+    chosen = (ids == at).astype(F32).astype(BF16)
     for copy in lined:
         copy.wait()
     rows_high, rows_low = pieces(rows[...])
@@ -155,24 +167,25 @@
         out_ref[:, h * group : (h + 1) * group, c : c + tile] = total.reshape(slices, group, tile)
 
 
-def partial_scores(recv, order, stored, slices):
-    queries, per, rank = recv.shape
+def partial_scores(recv, swapped, order, stored, slices):
+    held, per, rank = recv.shape
+    queries = CORES * held
     store, layers, _ = stored.shape
     sub = 8
     half = store * (queries // slices) // sub
     return pl.pallas_call(
         functools.partial(scores_kernel, layers),
-        in_specs=[WHOLE] * 3,
+        in_specs=[WHOLE] * 4,
         out_specs=WHOLE,
         out_shape=pltpu.VMEM((slices, sub, half), F32),
         scratch_shapes=[
             pltpu.VMEM((queries, per * rank), F32),
             pltpu.VMEM((2 * queries, per * rank), BF16),
-            pltpu.SemaphoreType.DMA((per,)),
+            pltpu.SemaphoreType.DMA((CORES, per)),
         ],
         compiler_params=limit(4),
         name="scores",
-    )(near(recv), order.reshape(1, queries), near(tiles_view(stored)))
+    )(near(recv), near(swapped), order.reshape(1, queries), near(tiles_view(stored)))
 
 
 def sum_kernel(parts_ref, out_ref):
@@ -195,12 +208,14 @@
     )(near(parts))
 
 
-def per_device(rows, slices, activations, out_grads, proj_in, proj_out, inv_in, inv_out, stored, query_order):
+def per_device(slices, activations, out_grads, proj_in, proj_out, inv_in, inv_out, stored, query_order):
     acts_low, grads_low = projected(activations, out_grads, proj_in, proj_out)
-    mine = preconditioned(acts_low, grads_low, inv_in, inv_out, rows, slices)
-    mine = mine.reshape((rows * slices,) + mine.shape[2:])
-    recv = lax.all_to_all(mine, ("row", "feat"), 0, 0, tiled=True)
-    parts = partial_scores(recv, query_order, stored, slices)
+    mine = preconditioned(acts_low, grads_low, inv_in, inv_out, ROWS // CORES, slices)
+    mine = mine.reshape((-1,) + mine.shape[2:])
+    alike = [[r * slices + f for r in range(c, ROWS, CORES) for f in range(slices)] for c in range(CORES)]
+    recv = lax.all_to_all(mine, ("row", "feat"), 0, 0, tiled=True, axis_index_groups=alike)
+    swapped = lax.ppermute(recv, "row", [(r, r ^ 1) for r in range(ROWS)])
+    parts = partial_scores(recv, swapped, query_order, stored, slices)
     return sum_parts(lax.all_to_all(parts, "feat", 0, 0, tiled=True))
 
 
@@ -216,7 +231,7 @@
         P(),
     )
     return jax.shard_map(
-        functools.partial(per_device, mesh.shape["row"], mesh.shape["feat"]),
+        functools.partial(per_device, mesh.shape["feat"]),
         mesh=mesh,
         in_specs=placed,
         out_specs=P("feat", "row"),

time: 64.3 us -> 61.6 us (0.958)
  blocking collectives: 51.9 us -> 47.1 us
  waiting for transfers between devices: 0 us -> 1.91 us
    all_to_all x1, blocking collectives: 28.9 us -> 24.9 us  [per_device(): lax.all_to_all(mine, ('row', 'feat'), 0, 0, tiled=True, axis_index_groups...]
    ppermute x0 -> x1, waiting for transfers between devices: none -> 1.91 us  [per_device(): swapped = lax.ppermute(recv, 'row', [(r, r ^ 1) for r in range(ROWS)])]
    all_to_all x1, blocking collectives: 23 us -> 22.2 us  [per_device(): return sum_parts(lax.all_to_all(parts, 'feat', 0, 0, tiled=True))]
  transfers between devices with their start and end apart: 0 -> 1, of which waited for: 0 -> 1; matrix products, arithmetic and copies ran while one was open for 0% -> 0% of each run, Pallas kernels for 0% -> 0%
where the time goes in v4:
time: 61.6 us; the launch traced here: 61.5 us
  blocking collectives  47.1 us (76%)
  Pallas kernels  12.3 us (20%)
  waiting for transfers between devices  1.91 us (3%)
    all_to_all x1, blocking collectives, per_device(): lax.all_to_all(mine, ('row', 'feat'), 0, 0, tiled=True, axis_index_groups...  24.9 us
    all_to_all x1, blocking collectives, per_device(): return sum_parts(lax.all_to_all(parts, 'feat', 0, 0, tiled=True))  22.2 us
    pallas_call x1, Pallas kernels, partial_scores(): pl.pallas_call(functools.partial(scores_kernel, layers), in_specs=[WHOLE]...  6.77 us
    pallas_call x1, Pallas kernels, projected(): pl.pallas_call(project_kernel, in_specs=[ANYWHERE] * 4, out_specs=[WHOLE]...  4.02 us
    ppermute x1, waiting for transfers between devices, per_device(): swapped = lax.ppermute(recv, 'row', [(r, r ^ 1) for r in range(ROWS)])  1.91 us
  transfers between devices with their start and end apart: 1, of which 1 were waited for; matrix products, arithmetic and copies ran while one was open for 0% of the time, Pallas kernels for 0%

profile of v4, /device:TPU:0, one launch (start us, length us, event | category | flops | bytes accessed | tf_op | source)
XLA Modules:
  0.0 61.5 jit_solution(8947391717598901576)
XLA Ops:
  0.0 0.0 copy-start.2
  0.0 0.0 copy-start.1
  0.0 4.0 %projected.1 = (f32[128,128]{1,0:T(8,128)S(1)}, f32[128,128]{1,0:T(8,128)S(1)}) custom-call(f32[4,32,4096]{2,1,0:T(8,128)} %acts_hbm.1, f32[4096,128]{1,0:T(8,128)} %pin_hbm.1, f32[4,32,4096]{2,1,0:T(8,128)} %grads_hbm.1, f32[4096,128]{1,0:T(8,128)} %pout_hbm.1), custom_call_target="tpu_custom_call" | custom-call | tf_op jit(solution)/shard_map/projected/pallas_call | solution.py:82
  4.0 0.0 slice-start
  4.0 0.0 copy-done.2
  4.1 0.0 copy-done.1
  4.1 0.0 slice-start.1
  4.1 0.0 slice-start.2
  4.1 0.0 slice-start.3
  4.1 0.0 copy-start
  4.1 0.9 %precond.1 = f32[2,32,16,128]{3,2,1,0:T(8,128)S(1)} custom-call(f32[128,128]{1,0:T(8,128)S(1)} %get-tuple-element.7.acts_low, f32[128,128]{1,0:T(8,128)S(1)} %get-tuple-element.8.grads_low, f32[4,128,128]{2,1,0:T(8,128)S(1)} %copy-done.1, f32[4,128,128]{2,1,0:T(8,128)S(1)} %copy-done.2), custom_call_target="tpu_custom_call" | custom-call | flops 8589934592 | bytes 1048576 | tf_op jit(solution)/shard_map/precond/pallas_call | solution.py:112
  5.0 24.9 %all_to_all.10.recv_ref = f32[64,16,128]{2,1,0:T(8,128)S(1)} all-to-all(f32[64,16,128]{2,1,0:T(8,128)S(1)} %bitcast.10), channel_id=1, replica_groups={{0,1,2,3,4,5,6,7,8,9,10,11,12,13,14,15,16,17,18,19,20,21,22,23,24,25,26..., dimensions={0} | all-to-all | bytes 1048576 | tf_op jit(solution)/shard_map/all_to_all | solution.py:216
  29.9 0.0 collective-permute-start
  29.9 1.9 %collective-permute-done.swapped_ref = f32[64,16,128]{2,1,0:T(8,128)S(1)} collective-permute-done((f32[64,16,128]{2,1,0:T(8,128)S(1)}, f32[64,16,128]{2,1,0:T(8,128)S(1)}, u32[]{:S(2)}, u32[]{:S(2)}) %collective-permute-start) | collective-permute-done | bytes 524320 | tf_op jit(solution)/shard_map/ppermute | solution.py:217
  31.8 0.0 slice-done
  31.8 0.0 slice-done.1
  31.8 0.0 slice-done.2
  31.8 0.0 slice-done.3
  31.9 0.0 copy-done
  31.9 6.8 %scores.1 = f32[32,8,1024]{2,1,0:T(8,128)S(1)} custom-call(f32[64,16,128]{2,1,0:T(8,128)S(1)} %all_to_all.10.recv_ref, f32[64,16,128]{2,1,0:T(8,128)S(1)} %collective-permute-done.swapped_ref, s32[1,128]{1,0:T(1,128)S(1)} %bitcast.11, f32[2048,16,128]{2,1,0:T(8,128)S(1)} %bitcast.9), custom_call_target="tpu_custom_call" | custom-call | tf_op jit(solution)/shard_map/scores/pallas_call | solution.py:176
  38.6 22.2 %all_to_all.11.parts_ref = f32[32,8,1024]{2,1,0:T(8,128)S(1)} all-to-all(f32[32,8,1024]{2,1,0:T(8,128)S(1)} %scores.1), channel_id=1, replica_groups=mesh['row'=4,'feat'=32] {'feat'}, dimensions={0} | all-to-all | bytes 2097152 | tf_op jit(solution)/shard_map/all_to_all | solution.py:219
  60.8 0.7 %sum_parts.1 = f32[4,2048]{1,0:T(4,128)} custom-call(f32[32,8,1024]{2,1,0:T(8,128)S(1)} %all_to_all.11.parts_ref), custom_call_target="tpu_custom_call" | custom-call | tf_op jit(solution)/shard_map/sum_parts/pallas_call | solution.py:202
  (1 shorter events, 0.0 us)
Async XLA Ops:
  0.0 4.0 %copy-start.2 = (f32[4,128,128]{2,1,0:T(8,128)S(1)}, f32[4,128,128]{2,1,0:T(8,128)}, u32[]{:S(2)}) copy-start(f32[4,128,128]{2,1,0:T(8,128)} %iout.1) | copy-start | bytes 786436
  0.0 4.1 %copy-start.1 = (f32[4,128,128]{2,1,0:T(8,128)S(1)}, f32[4,128,128]{2,1,0:T(8,128)}, u32[]{:S(2)}) copy-start(f32[4,128,128]{2,1,0:T(8,128)} %iin.1) | copy-start | bytes 786436
  4.0 27.8 %slice-start = ((s8[16777216]{0:T(1024)(128)(4,1)}), s8[4194304]{0:T(1024)(128)(4,1)S(1)}, s32[]{:S(2)}) async-start(s8[16777216]{0:T(1024)(128)(4,1)} %bitcast.7), calls=%async_computation.2 | async-start | bytes 8388608
  4.1 27.8 %slice-start.1 = ((s8[16777216]{0:T(1024)(128)(4,1)}), s8[4194304]{0:T(1024)(128)(4,1)S(1)}, s32[]{:S(2)}) async-start(s8[16777216]{0:T(1024)(128)(4,1)} %bitcast.7), calls=%async_computation.3 | async-start | bytes 8388608
  4.1 27.8 %slice-start.2 = ((s8[16777216]{0:T(1024)(128)(4,1)}), s8[4194304]{0:T(1024)(128)(4,1)S(1)}, s32[]{:S(2)}) async-start(s8[16777216]{0:T(1024)(128)(4,1)} %bitcast.7), calls=%async_computation.4 | async-start | bytes 8388608
  4.1 27.8 %slice-start.3 = ((s8[16777216]{0:T(1024)(128)(4,1)}), s8[4194304]{0:T(1024)(128)(4,1)S(1)}, s32[]{:S(2)}) async-start(s8[16777216]{0:T(1024)(128)(4,1)} %bitcast.7), calls=%async_computation.5 | async-start | bytes 8388608
  4.1 27.8 %copy-start = (s32[128]{0:T(128)S(1)}, s32[128]{0:T(128)}, u32[]{:S(2)}) copy-start(s32[128]{0:T(128)} %param.15) | copy-start | bytes 1540
  29.9 1.9 %collective-permute-start = (f32[64,16,128]{2,1,0:T(8,128)S(1)}, f32[64,16,128]{2,1,0:T(8,128)S(1)}, u32[]{:S(2)}, u32[]{:S(2)}) collective-permute-start(f32[64,16,128]{2,1,0:T(8,128)S(1)} %all_to_all.10.recv_ref), channel_id=1, source_target_pairs={{0,32},{32,0},{64,96},{96,64},{1,33},{33,1},{65,97},{97,65},{2,34}... | collective-permute-start | bytes 1572872 | tf_op jit(solution)/shard_map/ppermute | solution.py:217

commit v5 on v4

--- a/solution.py
+++ b/solution.py
@@ -94,7 +94,8 @@
     rows, slices, per, rank = out_ref.shape
     layers = iin.shape[0]
     tok = acts_low.shape[0] // layers
-    per = per // layers
+    runs = per // layers
+    each = []
     for l in range(layers):
         mine = slice(l * tok, (l + 1) * tok)
         right = wide_product(acts_low[mine, :], iin[l])
@@ -102,9 +103,10 @@
         (left_high, left_low), (right_high, right_low) = pieces(left), pieces(right)
         tall = jnp.concatenate([left_low, left_low, left_high, left_high], axis=0)
         other = jnp.concatenate([right_low, right_high, right_low, right_high], axis=0)
-        cond = dot(tall, other, TN).reshape(slices, per, rank)
-        for r in range(rows):
-            out_ref[r, :, l * per : (l + 1) * per, :] = cond
+        each.append(dot(tall, other, TN).reshape(slices, runs, 1, rank))
+    cond = jnp.concatenate(each, axis=2).reshape(slices, per, rank)
+    for r in range(rows):
+        out_ref[r] = cond
 
 
 def preconditioned(acts_low, grads_low, inv_in, inv_out, rows, slices):
@@ -134,28 +136,18 @@
     return (other * pairs + lax.shift_right_logical(row, CORES.bit_length() - 1)) * slices + (order & (slices - 1))
 
 
-def scores_kernel(layers, recv_ref, swapped_ref, order_ref, tiles_ref, out_ref, rows, picked, sems):
+def scores_kernel(recv_ref, swapped_ref, order_ref, tiles_ref, out_ref, picked):
     held, per, rank = recv_ref.shape
     queries = CORES * held
     slices, sub, half = out_ref.shape
     group = queries // slices
     store = tiles_ref.shape[0]
-    runs = per // layers
     tile = 256
-    lined = []
-    for t in range(per):
-        place = (t % runs) * layers + t // runs
-        for c, part in enumerate((recv_ref, swapped_ref)):
-            to = rows.at[pl.ds(c * held, held), pl.ds(place * rank, rank)]
-            lined.append(pltpu.make_async_copy(part.at[:, t, :], to, sems.at[c, t]))
-    for copy in lined:
-        copy.start()
     ids = lax.broadcasted_iota(jnp.int32, (queries, queries), 0)
     at = positions(order_ref[...], slices, lax.rem(lax.axis_index("row"), CORES))
     chosen = (ids == at).astype(F32).astype(BF16)
-    for copy in lined:
-        copy.wait()
-    rows_high, rows_low = pieces(rows[...])
+    rows = jnp.concatenate([ref[...].reshape(held, per * rank) for ref in (recv_ref, swapped_ref)], axis=0)
+    rows_high, rows_low = pieces(rows)
     picked[:queries, :] = dot(chosen, rows_high, TN).astype(BF16)
     picked[queries:, :] = dot(chosen, rows_low, TN).astype(BF16)
     for n in range(store // tile):
@@ -170,19 +162,15 @@
 def partial_scores(recv, swapped, order, stored, slices):
     held, per, rank = recv.shape
     queries = CORES * held
-    store, layers, _ = stored.shape
+    store = stored.shape[0]
     sub = 8
     half = store * (queries // slices) // sub
     return pl.pallas_call(
-        functools.partial(scores_kernel, layers),
+        scores_kernel,
         in_specs=[WHOLE] * 4,
         out_specs=WHOLE,
         out_shape=pltpu.VMEM((slices, sub, half), F32),
-        scratch_shapes=[
-            pltpu.VMEM((queries, per * rank), F32),
-            pltpu.VMEM((2 * queries, per * rank), BF16),
-            pltpu.SemaphoreType.DMA((CORES, per)),
-        ],
+        scratch_shapes=[pltpu.VMEM((2 * queries, per * rank), BF16)],
         compiler_params=limit(4),
         name="scores",
     )(near(recv), near(swapped), order.reshape(1, queries), near(tiles_view(stored)))

time: 61.6 us -> 60.8 us (0.987)
  Pallas kernels: 12.3 us -> 11.5 us
    pallas_call x1, Pallas kernels: 6.77 us -> 5.78 us  [partial_scores(): pl.pallas_call(scores_kernel, in_specs=[WHOLE] * 4, out_specs=WHOLE, out_...]
where the time goes in v5:
time: 60.8 us; the launch traced here: 60.6 us
  blocking collectives  47.1 us (77%)
  Pallas kernels  11.5 us (19%)
  waiting for transfers between devices  1.91 us (3%)
    all_to_all x1, blocking collectives, per_device(): lax.all_to_all(mine, ('row', 'feat'), 0, 0, tiled=True, axis_index_groups...  24.9 us
    all_to_all x1, blocking collectives, per_device(): return sum_parts(lax.all_to_all(parts, 'feat', 0, 0, tiled=True))  22.2 us
    pallas_call x1, Pallas kernels, partial_scores(): pl.pallas_call(scores_kernel, in_specs=[WHOLE] * 4, out_specs=WHOLE, out_...  5.78 us
    pallas_call x1, Pallas kernels, projected(): pl.pallas_call(project_kernel, in_specs=[ANYWHERE] * 4, out_specs=[WHOLE]...  4.02 us
    ppermute x1, waiting for transfers between devices, per_device(): swapped = lax.ppermute(recv, 'row', [(r, r ^ 1) for r in range(ROWS)])  1.91 us
  transfers between devices with their start and end apart: 1, of which 1 were waited for; matrix products, arithmetic and copies ran while one was open for 0% of the time, Pallas kernels for 0%

profile of v5, /device:TPU:0, one launch (start us, length us, event | category | flops | bytes accessed | tf_op | source)
XLA Modules:
  0.0 60.6 jit_solution(15698881435469396603)
XLA Ops:
  0.0 0.0 copy-start.2
  0.0 0.0 copy-start.1
  0.0 4.0 %projected.1 = (f32[128,128]{1,0:T(8,128)S(1)}, f32[128,128]{1,0:T(8,128)S(1)}) custom-call(f32[4,32,4096]{2,1,0:T(8,128)} %acts_hbm.1, f32[4096,128]{1,0:T(8,128)} %pin_hbm.1, f32[4,32,4096]{2,1,0:T(8,128)} %grads_hbm.1, f32[4096,128]{1,0:T(8,128)} %pout_hbm.1), custom_call_target="tpu_custom_call" | custom-call | tf_op jit(solution)/shard_map/projected/pallas_call | solution.py:82
  4.0 0.0 slice-start
  4.0 0.0 copy-done.2
  4.1 0.0 copy-done.1
  4.1 0.0 slice-start.1
  4.1 0.0 slice-start.2
  4.1 0.0 slice-start.3
  4.1 0.0 copy-start
  4.1 1.0 %precond.1 = f32[2,32,16,128]{3,2,1,0:T(8,128)S(1)} custom-call(f32[128,128]{1,0:T(8,128)S(1)} %get-tuple-element.7.acts_low, f32[128,128]{1,0:T(8,128)S(1)} %get-tuple-element.8.grads_low, f32[4,128,128]{2,1,0:T(8,128)S(1)} %copy-done.1, f32[4,128,128]{2,1,0:T(8,128)S(1)} %copy-done.2), custom_call_target="tpu_custom_call" | custom-call | flops 8589934592 | bytes 1048576 | tf_op jit(solution)/shard_map/precond/pallas_call | solution.py:114
  5.1 24.9 %all_to_all.10.recv_ref = f32[64,16,128]{2,1,0:T(8,128)S(1)} all-to-all(f32[64,16,128]{2,1,0:T(8,128)S(1)} %bitcast.10), channel_id=1, replica_groups={{0,1,2,3,4,5,6,7,8,9,10,11,12,13,14,15,16,17,18,19,20,21,22,23,24,25,26..., dimensions={0} | all-to-all | bytes 1048576 | tf_op jit(solution)/shard_map/all_to_all | solution.py:204
  30.1 0.0 collective-permute-start
  30.1 1.9 %collective-permute-done.swapped_ref = f32[64,16,128]{2,1,0:T(8,128)S(1)} collective-permute-done((f32[64,16,128]{2,1,0:T(8,128)S(1)}, f32[64,16,128]{2,1,0:T(8,128)S(1)}, u32[]{:S(2)}, u32[]{:S(2)}) %collective-permute-start) | collective-permute-done | bytes 524320 | tf_op jit(solution)/shard_map/ppermute | solution.py:205
  32.0 0.0 slice-done
  32.0 0.0 slice-done.1
  32.0 0.0 slice-done.2
  32.0 0.0 slice-done.3
  32.0 0.0 copy-done
  32.0 5.8 %scores.1 = f32[32,8,1024]{2,1,0:T(8,128)S(1)} custom-call(f32[64,16,128]{2,1,0:T(8,128)S(1)} %all_to_all.10.recv_ref, f32[64,16,128]{2,1,0:T(8,128)S(1)} %collective-permute-done.swapped_ref, s32[1,128]{1,0:T(1,128)S(1)} %bitcast.11, f32[2048,16,128]{2,1,0:T(8,128)S(1)} %bitcast.9), custom_call_target="tpu_custom_call" | custom-call | tf_op jit(solution)/shard_map/scores/pallas_call | solution.py:168
  37.8 22.2 %all_to_all.11.parts_ref = f32[32,8,1024]{2,1,0:T(8,128)S(1)} all-to-all(f32[32,8,1024]{2,1,0:T(8,128)S(1)} %scores.1), channel_id=1, replica_groups=mesh['row'=4,'feat'=32] {'feat'}, dimensions={0} | all-to-all | bytes 2097152 | tf_op jit(solution)/shard_map/all_to_all | solution.py:207
  60.0 0.7 %sum_parts.1 = f32[4,2048]{1,0:T(4,128)} custom-call(f32[32,8,1024]{2,1,0:T(8,128)S(1)} %all_to_all.11.parts_ref), custom_call_target="tpu_custom_call" | custom-call | tf_op jit(solution)/shard_map/sum_parts/pallas_call | solution.py:190
  (1 shorter events, 0.0 us)
Async XLA Ops:
  0.0 4.0 %copy-start.2 = (f32[4,128,128]{2,1,0:T(8,128)S(1)}, f32[4,128,128]{2,1,0:T(8,128)}, u32[]{:S(2)}) copy-start(f32[4,128,128]{2,1,0:T(8,128)} %iout.1) | copy-start | bytes 786436
  0.0 4.1 %copy-start.1 = (f32[4,128,128]{2,1,0:T(8,128)S(1)}, f32[4,128,128]{2,1,0:T(8,128)}, u32[]{:S(2)}) copy-start(f32[4,128,128]{2,1,0:T(8,128)} %iin.1) | copy-start | bytes 786436
  4.0 27.9 %slice-start = ((s8[16777216]{0:T(1024)(128)(4,1)}), s8[4194304]{0:T(1024)(128)(4,1)S(1)}, s32[]{:S(2)}) async-start(s8[16777216]{0:T(1024)(128)(4,1)} %bitcast.7), calls=%async_computation.2 | async-start | bytes 8388608
  4.1 27.9 %slice-start.1 = ((s8[16777216]{0:T(1024)(128)(4,1)}), s8[4194304]{0:T(1024)(128)(4,1)S(1)}, s32[]{:S(2)}) async-start(s8[16777216]{0:T(1024)(128)(4,1)} %bitcast.7), calls=%async_computation.3 | async-start | bytes 8388608
  4.1 27.9 %slice-start.2 = ((s8[16777216]{0:T(1024)(128)(4,1)}), s8[4194304]{0:T(1024)(128)(4,1)S(1)}, s32[]{:S(2)}) async-start(s8[16777216]{0:T(1024)(128)(4,1)} %bitcast.7), calls=%async_computation.4 | async-start | bytes 8388608
  4.1 27.9 %slice-start.3 = ((s8[16777216]{0:T(1024)(128)(4,1)}), s8[4194304]{0:T(1024)(128)(4,1)S(1)}, s32[]{:S(2)}) async-start(s8[16777216]{0:T(1024)(128)(4,1)} %bitcast.7), calls=%async_computation.5 | async-start | bytes 8388608
  4.1 27.9 %copy-start = (s32[128]{0:T(128)S(1)}, s32[128]{0:T(128)}, u32[]{:S(2)}) copy-start(s32[128]{0:T(128)} %param.15) | copy-start | bytes 1540
  30.1 1.9 %collective-permute-start = (f32[64,16,128]{2,1,0:T(8,128)S(1)}, f32[64,16,128]{2,1,0:T(8,128)S(1)}, u32[]{:S(2)}, u32[]{:S(2)}) collective-permute-start(f32[64,16,128]{2,1,0:T(8,128)S(1)} %all_to_all.10.recv_ref), channel_id=1, source_target_pairs={{0,32},{32,0},{64,96},{96,64},{1,33},{33,1},{65,97},{97,65},{2,34}... | collective-permute-start | bytes 1572872 | tf_op jit(solution)/shard_map/ppermute | solution.py:205

commit v6 on v5

--- a/solution.py
+++ b/solution.py
@@ -91,7 +91,8 @@
 
 
 def precond_kernel(acts_low, grads_low, iin, iout, out_ref):
-    rows, slices, per, rank = out_ref.shape
+    rows, slices, part, rank = out_ref.shape
+    per = CORES * part
     layers = iin.shape[0]
     tok = acts_low.shape[0] // layers
     runs = per // layers
@@ -106,7 +107,8 @@
         each.append(dot(tall, other, TN).reshape(slices, runs, 1, rank))
     cond = jnp.concatenate(each, axis=2).reshape(slices, per, rank)
     for r in range(rows):
-        out_ref[r] = cond
+        c = r % CORES
+        out_ref[r] = cond[:, c * part : (c + 1) * part, :]
 
 
 def preconditioned(acts_low, grads_low, inv_in, inv_out, rows, slices):
@@ -115,7 +117,7 @@
         precond_kernel,
         in_specs=[WHOLE] * 4,
         out_specs=WHOLE,
-        out_shape=pltpu.VMEM((rows, slices, layers * (rank // slices), rank), F32),
+        out_shape=pltpu.VMEM((rows, slices, layers * (rank // slices) // CORES, rank), F32),
         compiler_params=limit(4),
         cost_estimate=pl.CostEstimate(flops=1 << 33, bytes_accessed=1 << 20, transcendentals=0),
         name="precond",
@@ -128,52 +130,75 @@
     return stored.reshape(store, layers, runs, lanes).transpose(0, 2, 1, 3).reshape(store, runs * layers, lanes)
 
 
-def positions(order, slices, mine):
-    bits = slices.bit_length() - 1
-    row = lax.shift_right_logical(order, bits)
-    other = jnp.where((row & (CORES - 1)) == mine, 0, 1)
-    pairs = ROWS // CORES
-    return (other * pairs + lax.shift_right_logical(row, CORES.bit_length() - 1)) * slices + (order & (slices - 1))
-
-
-def scores_kernel(recv_ref, swapped_ref, order_ref, tiles_ref, out_ref, picked):
-    held, per, rank = recv_ref.shape
-    queries = CORES * held
-    slices, sub, half = out_ref.shape
-    group = queries // slices
+def half_scores(recv_ref, order_ref, tiles_ref, picked, side, emit):
+    queries, part, rank = recv_ref.shape
     store = tiles_ref.shape[0]
+    width = part * rank
     tile = 256
     ids = lax.broadcasted_iota(jnp.int32, (queries, queries), 0)
-    at = positions(order_ref[...], slices, lax.rem(lax.axis_index("row"), CORES))
-    chosen = (ids == at).astype(F32).astype(BF16)
-    rows = jnp.concatenate([ref[...].reshape(held, per * rank) for ref in (recv_ref, swapped_ref)], axis=0)
-    rows_high, rows_low = pieces(rows)
+    chosen = (ids == order_ref[...]).astype(F32).astype(BF16)
+    rows_high, rows_low = pieces(recv_ref[...].reshape(queries, width))
     picked[:queries, :] = dot(chosen, rows_high, TN).astype(BF16)
     picked[queries:, :] = dot(chosen, rows_low, TN).astype(BF16)
+    here = pl.ds(pl.multiple_of(side * part, part), part)
     for n in range(store // tile):
-        high, low = pieces(tiles_ref[n * tile : (n + 1) * tile].reshape(tile, per * rank))
+        at = slice(n * tile, (n + 1) * tile)
+        high, low = pieces(tiles_ref[at, here, :].reshape(tile, width))
         wide = dot(high, picked[...], NT)
         narrow = dot(low, picked[:queries, :], NT)
-        total = (wide[:, :queries] + (wide[:, queries:] + narrow)).T
-        h, c = divmod(n * tile, half)
+        emit(n * tile, wide[:, :queries] + (wide[:, queries:] + narrow))
+
+
+def core_index():
+    return lax.rem(lax.axis_index("row"), CORES)
+
+
+def own_kernel(recv_ref, order_ref, tiles_ref, out_ref, picked):
+    def emit(start, scores):
+        out_ref[start : start + scores.shape[0], :] = scores
+
+    half_scores(recv_ref, order_ref, tiles_ref, picked, core_index(), emit)
+
+
+def other_kernel(swapped_ref, order_ref, tiles_ref, own_ref, out_ref, picked):
+    slices, sub, half = out_ref.shape
+    group = own_ref.shape[1] // slices
+
+    def emit(start, scores):
+        tile = scores.shape[0]
+        total = (scores + own_ref[start : start + tile, :]).T
+        h, c = divmod(start, half)
         out_ref[:, h * group : (h + 1) * group, c : c + tile] = total.reshape(slices, group, tile)
 
+    half_scores(swapped_ref, order_ref, tiles_ref, picked, CORES - 1 - core_index(), emit)
+
 
 def partial_scores(recv, swapped, order, stored, slices):
-    held, per, rank = recv.shape
-    queries = CORES * held
+    queries, part, rank = recv.shape
     store = stored.shape[0]
+    tiles = near(tiles_view(stored))
+    order = order.reshape(1, queries)
+    scratch = [pltpu.VMEM((2 * queries, part * rank), BF16)]
+    own = pl.pallas_call(
+        own_kernel,
+        in_specs=[WHOLE] * 3,
+        out_specs=WHOLE,
+        out_shape=pltpu.VMEM((store, queries), F32),
+        scratch_shapes=scratch,
+        compiler_params=limit(4),
+        cost_estimate=pl.CostEstimate(flops=3 * store * queries * part * rank, bytes_accessed=2 * store * part * rank, transcendentals=0),
+        name="own_half",
+    )(near(recv), order, tiles)
     sub = 8
-    half = store * (queries // slices) // sub
-    return pl.pallas_call(
-        scores_kernel,
+    return pl.pallas_call(
+        other_kernel,
         in_specs=[WHOLE] * 4,
         out_specs=WHOLE,
-        out_shape=pltpu.VMEM((slices, sub, half), F32),
-        scratch_shapes=[pltpu.VMEM((2 * queries, per * rank), BF16)],
+        out_shape=pltpu.VMEM((slices, sub, store * (queries // slices) // sub), F32),
+        scratch_shapes=scratch,
         compiler_params=limit(4),
-        name="scores",
-    )(near(recv), near(swapped), order.reshape(1, queries), near(tiles_view(stored)))
+        name="other_half",
+    )(near(swapped), order, tiles, near(own))
 
 
 def sum_kernel(parts_ref, out_ref):
@@ -198,10 +223,9 @@
 
 def per_device(slices, activations, out_grads, proj_in, proj_out, inv_in, inv_out, stored, query_order):
     acts_low, grads_low = projected(activations, out_grads, proj_in, proj_out)
-    mine = preconditioned(acts_low, grads_low, inv_in, inv_out, ROWS // CORES, slices)
+    mine = preconditioned(acts_low, grads_low, inv_in, inv_out, ROWS, slices)
     mine = mine.reshape((-1,) + mine.shape[2:])
-    alike = [[r * slices + f for r in range(c, ROWS, CORES) for f in range(slices)] for c in range(CORES)]
-    recv = lax.all_to_all(mine, ("row", "feat"), 0, 0, tiled=True, axis_index_groups=alike)
+    recv = lax.all_to_all(mine, ("row", "feat"), 0, 0, tiled=True)
     swapped = lax.ppermute(recv, "row", [(r, r ^ 1) for r in range(ROWS)])
     parts = partial_scores(recv, swapped, query_order, stored, slices)
     return sum_parts(lax.all_to_all(parts, "feat", 0, 0, tiled=True))

time: 60.8 us -> 59.3 us (0.975)
  waiting for transfers between devices: 1.91 us -> 0.01 us
  blocking collectives: 47.1 us -> 46.4 us
  Pallas kernels: 11.5 us -> 12.2 us
    ppermute x1, waiting for transfers between devices: 1.91 us -> 0.01 us  [per_device(): swapped = lax.ppermute(recv, 'row', [(r, r ^ 1) for r in range(ROWS)])]
    all_to_all x1, blocking collectives: 24.9 us -> 23.7 us  [per_device(): recv = lax.all_to_all(mine, ('row', 'feat'), 0, 0, tiled=True)]
    pallas_call x1 -> x2, Pallas kernels: 5.78 us -> 6.52 us  [the longest x1 3.36 us: partial_scores(): pl.pallas_call(other_kernel, in_specs=[WHOLE] * 4, out_specs=WHOLE, out_s...]
  transfers between devices with their start and end apart: 1 -> 1, of which waited for: 1 -> 0; matrix products, arithmetic and copies ran while one was open for 0% -> 0% of each run, Pallas kernels for 0% -> 5%
where the time goes in v6:
time: 59.3 us; the launch traced here: 59.2 us
  blocking collectives  46.4 us (78%)
  Pallas kernels  12.2 us (21%)
    all_to_all x1, blocking collectives, per_device(): recv = lax.all_to_all(mine, ('row', 'feat'), 0, 0, tiled=True)  23.7 us
    all_to_all x1, blocking collectives, per_device(): return sum_parts(lax.all_to_all(parts, 'feat', 0, 0, tiled=True))  22.6 us
    pallas_call x1, Pallas kernels, projected(): pl.pallas_call(project_kernel, in_specs=[ANYWHERE] * 4, out_specs=[WHOLE]...  4.02 us
    pallas_call x1, Pallas kernels, partial_scores(): pl.pallas_call(other_kernel, in_specs=[WHOLE] * 4, out_specs=WHOLE, out_s...  3.36 us
    pallas_call x1, Pallas kernels, partial_scores(): pl.pallas_call(own_kernel, in_specs=[WHOLE] * 3, out_specs=WHOLE, out_sha...  3.16 us
  transfers between devices with their start and end apart: 1, of which 0 were waited for; matrix products, arithmetic and copies ran while one was open for 0% of the time, Pallas kernels for 5%

profile of v6, /device:TPU:0, one launch (start us, length us, event | category | flops | bytes accessed | tf_op | source)
XLA Modules:
  0.0 59.2 jit_solution(14967560865613078829)
XLA Ops:
  0.0 0.0 copy-start.2
  0.0 0.0 copy-start.1
  0.0 4.0 %projected.1 = (f32[128,128]{1,0:T(8,128)S(1)}, f32[128,128]{1,0:T(8,128)S(1)}) custom-call(f32[4,32,4096]{2,1,0:T(8,128)} %acts_hbm.1, f32[4096,128]{1,0:T(8,128)} %pin_hbm.1, f32[4,32,4096]{2,1,0:T(8,128)} %grads_hbm.1, f32[4096,128]{1,0:T(8,128)} %pout_hbm.1), custom_call_target="tpu_custom_call" | custom-call | tf_op jit(solution)/shard_map/projected/pallas_call | solution.py:82
  4.0 0.0 slice-start
  4.0 0.0 copy-done.2
  4.1 0.0 copy-done.1
  4.1 0.0 slice-start.1
  4.1 0.0 slice-start.2
  4.1 0.0 slice-start.3
  4.1 0.0 copy-start
  4.1 1.0 %precond.1 = f32[4,32,8,128]{3,2,1,0:T(8,128)S(1)} custom-call(f32[128,128]{1,0:T(8,128)S(1)} %get-tuple-element.7.acts_low, f32[128,128]{1,0:T(8,128)S(1)} %get-tuple-element.8.grads_low, f32[4,128,128]{2,1,0:T(8,128)S(1)} %copy-done.1, f32[4,128,128]{2,1,0:T(8,128)S(1)} %copy-done.2), custom_call_target="tpu_custom_call" | custom-call | flops 8589934592 | bytes 1048576 | tf_op jit(solution)/shard_map/precond/pallas_call | solution.py:116
  5.1 23.7 %all_to_all.10.recv_ref = f32[128,8,128]{2,1,0:T(8,128)S(1)} all-to-all(f32[128,8,128]{2,1,0:T(8,128)S(1)} %bitcast.11), channel_id=1, replica_groups=mesh['row'=4,'feat'=32] {'row','feat'}, dimensions={0} | all-to-all | bytes 1048576 | tf_op jit(solution)/shard_map/all_to_all | solution.py:228
  28.8 0.4 collective-permute-start
  29.3 0.0 slice-done
  29.3 0.0 slice-done.1
  29.3 0.0 slice-done.2
  29.3 0.0 slice-done.3
  29.3 0.0 copy-done
  29.3 3.2 %own_half.1.own_ref = f32[2048,128]{1,0:T(8,128)S(1)} custom-call(f32[128,8,128]{2,1,0:T(8,128)S(1)} %all_to_all.10.recv_ref, s32[1,128]{1,0:T(1,128)S(1)} %bitcast.12, f32[2048,16,128]{2,1,0:T(8,128)S(1)} %bitcast.9), custom_call_target="tpu_custom_call" | custom-call | flops 805306368 | bytes 4194304 | tf_op jit(solution)/shard_map/own_half/pallas_call | solution.py:182
  32.5 0.0 collective-permute-done.swapped_ref
  32.5 3.4 %other_half.1 = f32[32,8,1024]{2,1,0:T(8,128)S(1)} custom-call(f32[128,8,128]{2,1,0:T(8,128)S(1)} %collective-permute-done.swapped_ref, s32[1,128]{1,0:T(1,128)S(1)} %bitcast.13, f32[2048,16,128]{2,1,0:T(8,128)S(1)} %bitcast.10, f32[2048,128]{1,0:T(8,128)S(1)} %own_half.1.own_ref), custom_call_target="tpu_custom_call" | custom-call | tf_op jit(solution)/shard_map/other_half/pallas_call | solution.py:193
  35.8 22.6 %all_to_all.11.parts_ref = f32[32,8,1024]{2,1,0:T(8,128)S(1)} all-to-all(f32[32,8,1024]{2,1,0:T(8,128)S(1)} %other_half.1), channel_id=1, replica_groups=mesh['row'=4,'feat'=32] {'feat'}, dimensions={0} | all-to-all | bytes 2097152 | tf_op jit(solution)/shard_map/all_to_all | solution.py:231
  58.5 0.7 %sum_parts.1 = f32[4,2048]{1,0:T(4,128)} custom-call(f32[32,8,1024]{2,1,0:T(8,128)S(1)} %all_to_all.11.parts_ref), custom_call_target="tpu_custom_call" | custom-call | tf_op jit(solution)/shard_map/sum_parts/pallas_call | solution.py:215
  (1 shorter events, 0.0 us)
Async XLA Ops:
  0.0 4.0 %copy-start.2 = (f32[4,128,128]{2,1,0:T(8,128)S(1)}, f32[4,128,128]{2,1,0:T(8,128)}, u32[]{:S(2)}) copy-start(f32[4,128,128]{2,1,0:T(8,128)} %iout.1) | copy-start | bytes 786436
  0.0 4.1 %copy-start.1 = (f32[4,128,128]{2,1,0:T(8,128)S(1)}, f32[4,128,128]{2,1,0:T(8,128)}, u32[]{:S(2)}) copy-start(f32[4,128,128]{2,1,0:T(8,128)} %iin.1) | copy-start | bytes 786436
  4.0 25.2 %slice-start = ((s8[16777216]{0:T(1024)(128)(4,1)}), s8[4194304]{0:T(1024)(128)(4,1)S(1)}, s32[]{:S(2)}) async-start(s8[16777216]{0:T(1024)(128)(4,1)} %bitcast.7), calls=%async_computation.2 | async-start | bytes 8388608
  4.1 25.2 %slice-start.1 = ((s8[16777216]{0:T(1024)(128)(4,1)}), s8[4194304]{0:T(1024)(128)(4,1)S(1)}, s32[]{:S(2)}) async-start(s8[16777216]{0:T(1024)(128)(4,1)} %bitcast.7), calls=%async_computation.3 | async-start | bytes 8388608
  4.1 25.2 %slice-start.2 = ((s8[16777216]{0:T(1024)(128)(4,1)}), s8[4194304]{0:T(1024)(128)(4,1)S(1)}, s32[]{:S(2)}) async-start(s8[16777216]{0:T(1024)(128)(4,1)} %bitcast.7), calls=%async_computation.4 | async-start | bytes 8388608
  4.1 25.2 %slice-start.3 = ((s8[16777216]{0:T(1024)(128)(4,1)}), s8[4194304]{0:T(1024)(128)(4,1)S(1)}, s32[]{:S(2)}) async-start(s8[16777216]{0:T(1024)(128)(4,1)} %bitcast.7), calls=%async_computation.5 | async-start | bytes 8388608
  4.1 25.2 %copy-start = (s32[128]{0:T(128)S(1)}, s32[128]{0:T(128)}, u32[]{:S(2)}) copy-start(s32[128]{0:T(128)} %param.15) | copy-start | bytes 1540
  28.8 3.6 %collective-permute-start = (f32[128,8,128]{2,1,0:T(8,128)S(1)}, f32[128,8,128]{2,1,0:T(8,128)S(1)}, u32[]{:S(2)}, u32[]{:S(2)}) collective-permute-start(f32[128,8,128]{2,1,0:T(8,128)S(1)} %all_to_all.10.recv_ref), channel_id=1, source_target_pairs={{0,32},{32,0},{64,96},{96,64},{1,33},{33,1},{65,97},{97,65},{2,34}... | collective-permute-start | bytes 1572872 | tf_op jit(solution)/shard_map/ppermute | solution.py:229

commit v7 on v6

--- a/solution.py
+++ b/solution.py
@@ -96,7 +96,7 @@
     layers = iin.shape[0]
     tok = acts_low.shape[0] // layers
     runs = per // layers
-    each = []
+    share = runs // CORES
     for l in range(layers):
         mine = slice(l * tok, (l + 1) * tok)
         right = wide_product(acts_low[mine, :], iin[l])
@@ -104,11 +104,10 @@
         (left_high, left_low), (right_high, right_low) = pieces(left), pieces(right)
         tall = jnp.concatenate([left_low, left_low, left_high, left_high], axis=0)
         other = jnp.concatenate([right_low, right_high, right_low, right_high], axis=0)
-        each.append(dot(tall, other, TN).reshape(slices, runs, 1, rank))
-    cond = jnp.concatenate(each, axis=2).reshape(slices, per, rank)
-    for r in range(rows):
-        c = r % CORES
-        out_ref[r] = cond[:, c * part : (c + 1) * part, :]
+        cond = dot(tall, other, TN).reshape(slices, runs, rank)
+        for r in range(rows):
+            c = r % CORES
+            out_ref[r, :, l * share : (l + 1) * share, :] = cond[:, c * share : (c + 1) * share, :]
 
 
 def preconditioned(acts_low, grads_low, inv_in, inv_out, rows, slices):
@@ -130,14 +129,17 @@
     return stored.reshape(store, layers, runs, lanes).transpose(0, 2, 1, 3).reshape(store, runs * layers, lanes)
 
 
-def half_scores(recv_ref, order_ref, tiles_ref, picked, side, emit):
+def half_scores(layers, recv_ref, order_ref, tiles_ref, picked, side, emit):
     queries, part, rank = recv_ref.shape
     store = tiles_ref.shape[0]
     width = part * rank
-    tile = 256
+    tile = 1024
     ids = lax.broadcasted_iota(jnp.int32, (queries, queries), 0)
     chosen = (ids == order_ref[...]).astype(F32).astype(BF16)
-    rows_high, rows_low = pieces(recv_ref[...].reshape(queries, width))
+    rows = recv_ref[...].reshape(queries, width)
+    share = part // layers
+    blocks = [(l * share + run) * rank for run in range(share) for l in range(layers)]
+    rows_high, rows_low = pieces(jnp.concatenate([rows[:, b : b + rank] for b in blocks], axis=1))
     picked[:queries, :] = dot(chosen, rows_high, TN).astype(BF16)
     picked[queries:, :] = dot(chosen, rows_low, TN).astype(BF16)
     here = pl.ds(pl.multiple_of(side * part, part), part)
@@ -153,14 +155,14 @@
     return lax.rem(lax.axis_index("row"), CORES)
 
 
-def own_kernel(recv_ref, order_ref, tiles_ref, out_ref, picked):
+def own_kernel(layers, recv_ref, order_ref, tiles_ref, out_ref, picked):
     def emit(start, scores):
         out_ref[start : start + scores.shape[0], :] = scores
 
-    half_scores(recv_ref, order_ref, tiles_ref, picked, core_index(), emit)
-
-
-def other_kernel(swapped_ref, order_ref, tiles_ref, own_ref, out_ref, picked):
+    half_scores(layers, recv_ref, order_ref, tiles_ref, picked, core_index(), emit)
+
+
+def other_kernel(layers, swapped_ref, order_ref, tiles_ref, own_ref, out_ref, picked):
     slices, sub, half = out_ref.shape
     group = own_ref.shape[1] // slices
 
@@ -170,17 +172,17 @@
         h, c = divmod(start, half)
         out_ref[:, h * group : (h + 1) * group, c : c + tile] = total.reshape(slices, group, tile)
 
-    half_scores(swapped_ref, order_ref, tiles_ref, picked, CORES - 1 - core_index(), emit)
+    half_scores(layers, swapped_ref, order_ref, tiles_ref, picked, CORES - 1 - core_index(), emit)
 
 
 def partial_scores(recv, swapped, order, stored, slices):
     queries, part, rank = recv.shape
-    store = stored.shape[0]
+    store, layers, _ = stored.shape
     tiles = near(tiles_view(stored))
     order = order.reshape(1, queries)
     scratch = [pltpu.VMEM((2 * queries, part * rank), BF16)]
     own = pl.pallas_call(
-        own_kernel,
+        functools.partial(own_kernel, layers),
         in_specs=[WHOLE] * 3,
         out_specs=WHOLE,
         out_shape=pltpu.VMEM((store, queries), F32),
@@ -191,7 +193,7 @@
     )(near(recv), order, tiles)
     sub = 8
     return pl.pallas_call(
-        other_kernel,
+        functools.partial(other_kernel, layers),
         in_specs=[WHOLE] * 4,
         out_specs=WHOLE,
         out_shape=pltpu.VMEM((slices, sub, store * (queries // slices) // sub), F32),

time: 59.3 us -> 58.7 us (0.990)
  no operation moved by 1% of the time
where the time goes in v7:
time: 58.7 us; the launch traced here: 58.6 us
  blocking collectives  46.3 us (79%)
  Pallas kernels  11.7 us (20%)
    all_to_all x1, blocking collectives, per_device(): recv = lax.all_to_all(mine, ('row', 'feat'), 0, 0, tiled=True)  23.7 us
    all_to_all x1, blocking collectives, per_device(): return sum_parts(lax.all_to_all(parts, 'feat', 0, 0, tiled=True))  22.6 us
    pallas_call x1, Pallas kernels, projected(): pl.pallas_call(project_kernel, in_specs=[ANYWHERE] * 4, out_specs=[WHOLE]...  4.02 us
    pallas_call x1, Pallas kernels, partial_scores(): pl.pallas_call(functools.partial(other_kernel, layers), in_specs=[WHOLE]...  3.11 us
    pallas_call x1, Pallas kernels, partial_scores(): pl.pallas_call(functools.partial(own_kernel, layers), in_specs=[WHOLE] *...  2.94 us
  transfers between devices with their start and end apart: 1, of which 0 were waited for; matrix products, arithmetic and copies ran while one was open for 0% of the time, Pallas kernels for 5%

profile of v7, /device:TPU:0, one launch (start us, length us, event | category | flops | bytes accessed | tf_op | source)
XLA Modules:
  0.0 58.6 jit_solution(5809080802193807603)
XLA Ops:
  0.0 0.0 copy-start.2
  0.0 0.0 copy-start.1
  0.0 4.0 %projected.1 = (f32[128,128]{1,0:T(8,128)S(1)}, f32[128,128]{1,0:T(8,128)S(1)}) custom-call(f32[4,32,4096]{2,1,0:T(8,128)} %acts_hbm.1, f32[4096,128]{1,0:T(8,128)} %pin_hbm.1, f32[4,32,4096]{2,1,0:T(8,128)} %grads_hbm.1, f32[4096,128]{1,0:T(8,128)} %pout_hbm.1), custom_call_target="tpu_custom_call" | custom-call | tf_op jit(solution)/shard_map/projected/pallas_call | solution.py:82
  4.0 0.0 slice-start
  4.0 0.0 copy-done.2
  4.1 0.0 copy-done.1
  4.1 0.0 slice-start.1
  4.1 0.0 slice-start.2
  4.1 0.0 slice-start.3
  4.1 0.0 copy-start
  4.1 0.9 %precond.1 = f32[4,32,8,128]{3,2,1,0:T(8,128)S(1)} custom-call(f32[128,128]{1,0:T(8,128)S(1)} %get-tuple-element.7.acts_low, f32[128,128]{1,0:T(8,128)S(1)} %get-tuple-element.8.grads_low, f32[4,128,128]{2,1,0:T(8,128)S(1)} %copy-done.1, f32[4,128,128]{2,1,0:T(8,128)S(1)} %copy-done.2), custom_call_target="tpu_custom_call" | custom-call | flops 8589934592 | bytes 1048576 | tf_op jit(solution)/shard_map/precond/pallas_call | solution.py:115
  5.0 23.7 %all_to_all.10.recv_ref = f32[128,8,128]{2,1,0:T(8,128)S(1)} all-to-all(f32[128,8,128]{2,1,0:T(8,128)S(1)} %bitcast.11), channel_id=1, replica_groups=mesh['row'=4,'feat'=32] {'row','feat'}, dimensions={0} | all-to-all | bytes 1048576 | tf_op jit(solution)/shard_map/all_to_all | solution.py:230
  28.7 0.4 collective-permute-start
  29.1 0.0 slice-done
  29.1 0.0 slice-done.1
  29.2 0.0 slice-done.2
  29.2 0.0 slice-done.3
  29.2 0.0 copy-done
  29.2 2.9 %own_half.1.own_ref = f32[2048,128]{1,0:T(8,128)S(1)} custom-call(f32[128,8,128]{2,1,0:T(8,128)S(1)} %all_to_all.10.recv_ref, s32[1,128]{1,0:T(1,128)S(1)} %bitcast.12, f32[2048,16,128]{2,1,0:T(8,128)S(1)} %bitcast.9), custom_call_target="tpu_custom_call" | custom-call | flops 805306368 | bytes 4194304 | tf_op jit(solution)/shard_map/own_half/pallas_call | solution.py:184
  32.1 0.0 collective-permute-done.swapped_ref
  32.1 3.1 %other_half.1 = f32[32,8,1024]{2,1,0:T(8,128)S(1)} custom-call(f32[128,8,128]{2,1,0:T(8,128)S(1)} %collective-permute-done.swapped_ref, s32[1,128]{1,0:T(1,128)S(1)} %bitcast.13, f32[2048,16,128]{2,1,0:T(8,128)S(1)} %bitcast.10, f32[2048,128]{1,0:T(8,128)S(1)} %own_half.1.own_ref), custom_call_target="tpu_custom_call" | custom-call | tf_op jit(solution)/shard_map/other_half/pallas_call | solution.py:195
  35.3 22.6 %all_to_all.11.parts_ref = f32[32,8,1024]{2,1,0:T(8,128)S(1)} all-to-all(f32[32,8,1024]{2,1,0:T(8,128)S(1)} %other_half.1), channel_id=1, replica_groups=mesh['row'=4,'feat'=32] {'feat'}, dimensions={0} | all-to-all | bytes 2097152 | tf_op jit(solution)/shard_map/all_to_all | solution.py:233
  57.9 0.7 %sum_parts.1 = f32[4,2048]{1,0:T(4,128)} custom-call(f32[32,8,1024]{2,1,0:T(8,128)S(1)} %all_to_all.11.parts_ref), custom_call_target="tpu_custom_call" | custom-call | tf_op jit(solution)/shard_map/sum_parts/pallas_call | solution.py:217
  (1 shorter events, 0.0 us)
Async XLA Ops:
  0.0 4.0 %copy-start.2 = (f32[4,128,128]{2,1,0:T(8,128)S(1)}, f32[4,128,128]{2,1,0:T(8,128)}, u32[]{:S(2)}) copy-start(f32[4,128,128]{2,1,0:T(8,128)} %iout.1) | copy-start | bytes 786436
  0.0 4.1 %copy-start.1 = (f32[4,128,128]{2,1,0:T(8,128)S(1)}, f32[4,128,128]{2,1,0:T(8,128)}, u32[]{:S(2)}) copy-start(f32[4,128,128]{2,1,0:T(8,128)} %iin.1) | copy-start | bytes 786436
  4.0 25.1 %slice-start = ((s8[16777216]{0:T(1024)(128)(4,1)}), s8[4194304]{0:T(1024)(128)(4,1)S(1)}, s32[]{:S(2)}) async-start(s8[16777216]{0:T(1024)(128)(4,1)} %bitcast.7), calls=%async_computation.2 | async-start | bytes 8388608
  4.1 25.1 %slice-start.1 = ((s8[16777216]{0:T(1024)(128)(4,1)}), s8[4194304]{0:T(1024)(128)(4,1)S(1)}, s32[]{:S(2)}) async-start(s8[16777216]{0:T(1024)(128)(4,1)} %bitcast.7), calls=%async_computation.3 | async-start | bytes 8388608
  4.1 25.1 %slice-start.2 = ((s8[16777216]{0:T(1024)(128)(4,1)}), s8[4194304]{0:T(1024)(128)(4,1)S(1)}, s32[]{:S(2)}) async-start(s8[16777216]{0:T(1024)(128)(4,1)} %bitcast.7), calls=%async_computation.4 | async-start | bytes 8388608
  4.1 25.1 %slice-start.3 = ((s8[16777216]{0:T(1024)(128)(4,1)}), s8[4194304]{0:T(1024)(128)(4,1)S(1)}, s32[]{:S(2)}) async-start(s8[16777216]{0:T(1024)(128)(4,1)} %bitcast.7), calls=%async_computation.5 | async-start | bytes 8388608
  4.1 25.1 %copy-start = (s32[128]{0:T(128)S(1)}, s32[128]{0:T(128)}, u32[]{:S(2)}) copy-start(s32[128]{0:T(128)} %param.15) | copy-start | bytes 1540
  28.7 3.4 %collective-permute-start = (f32[128,8,128]{2,1,0:T(8,128)S(1)}, f32[128,8,128]{2,1,0:T(8,128)S(1)}, u32[]{:S(2)}, u32[]{:S(2)}) collective-permute-start(f32[128,8,128]{2,1,0:T(8,128)S(1)} %all_to_all.10.recv_ref), channel_id=1, source_target_pairs={{0,32},{32,0},{64,96},{96,64},{1,33},{33,1},{65,97},{97,65},{2,34}... | collective-permute-start | bytes 1572872 | tf_op jit(solution)/shard_map/ppermute | solution.py:231

commit v8 on v7

--- a/solution.py
+++ b/solution.py
@@ -74,7 +74,7 @@
     grads_low_ref[...] = grads_low
 
 
-def projected(activations, out_grads, proj_in, proj_out, count=4):
+def projected(activations, out_grads, proj_in, proj_out, count=8):
     layers, tok, width = activations.shape
     rank = proj_in.shape[1]
     tokens = pltpu.VMEM((layers, tok, width), F32)
@@ -97,10 +97,10 @@
     tok = acts_low.shape[0] // layers
     runs = per // layers
     share = runs // CORES
-    for l in range(layers):
-        mine = slice(l * tok, (l + 1) * tok)
-        right = wide_product(acts_low[mine, :], iin[l])
-        left = wide_product(grads_low[mine, :], iout[l], flip=True)
+    mine = [slice(l * tok, (l + 1) * tok) for l in range(layers)]
+    rights = [wide_product(acts_low[mine[l], :], iin[l]) for l in range(layers)]
+    lefts = [wide_product(grads_low[mine[l], :], iout[l], flip=True) for l in range(layers)]
+    for l, (left, right) in enumerate(zip(lefts, rights)):
         (left_high, left_low), (right_high, right_low) = pieces(left), pieces(right)
         tall = jnp.concatenate([left_low, left_low, left_high, left_high], axis=0)
         other = jnp.concatenate([right_low, right_high, right_low, right_high], axis=0)

time: 58.7 us -> 58.4 us (level)
  no operation moved by 1% of the time
where the time goes in v8:
time: 58.4 us; the launch traced here: 58.3 us
  blocking collectives  46.4 us (79%)
  Pallas kernels  11.4 us (20%)
    all_to_all x1, blocking collectives, per_device(): recv = lax.all_to_all(mine, ('row', 'feat'), 0, 0, tiled=True)  23.7 us
    all_to_all x1, blocking collectives, per_device(): return sum_parts(lax.all_to_all(parts, 'feat', 0, 0, tiled=True))  22.6 us
    pallas_call x1, Pallas kernels, projected(): pl.pallas_call(project_kernel, in_specs=[ANYWHERE] * 4, out_specs=[WHOLE]...  4.07 us
    pallas_call x1, Pallas kernels, partial_scores(): pl.pallas_call(functools.partial(other_kernel, layers), in_specs=[WHOLE]...  3.11 us
    pallas_call x1, Pallas kernels, partial_scores(): pl.pallas_call(functools.partial(own_kernel, layers), in_specs=[WHOLE] *...  2.94 us
  transfers between devices with their start and end apart: 1, of which 0 were waited for; matrix products, arithmetic and copies ran while one was open for 0% of the time, Pallas kernels for 5%

profile of v8, /device:TPU:0, one launch (start us, length us, event | category | flops | bytes accessed | tf_op | source)
XLA Modules:
  0.0 58.3 jit_solution(3969685891146282849)
XLA Ops:
  0.0 0.0 copy-start.2
  0.0 0.0 copy-start.1
  0.0 4.1 %projected.1 = (f32[128,128]{1,0:T(8,128)S(1)}, f32[128,128]{1,0:T(8,128)S(1)}) custom-call(f32[4,32,4096]{2,1,0:T(8,128)} %acts_hbm.1, f32[4096,128]{1,0:T(8,128)} %pin_hbm.1, f32[4,32,4096]{2,1,0:T(8,128)} %grads_hbm.1, f32[4096,128]{1,0:T(8,128)} %pout_hbm.1), custom_call_target="tpu_custom_call" | custom-call | tf_op jit(solution)/shard_map/projected/pallas_call | solution.py:82
  4.1 0.0 slice-start
  4.1 0.0 copy-done.2
  4.1 0.0 copy-done.1
  4.1 0.0 slice-start.1
  4.1 0.0 slice-start.2
  4.1 0.0 slice-start.3
  4.2 0.0 copy-start
  4.2 0.6 precond.1
  4.7 23.7 %all_to_all.10.recv_ref = f32[128,8,128]{2,1,0:T(8,128)S(1)} all-to-all(f32[128,8,128]{2,1,0:T(8,128)S(1)} %bitcast.11), channel_id=1, replica_groups=mesh['row'=4,'feat'=32] {'row','feat'}, dimensions={0} | all-to-all | bytes 1048576 | tf_op jit(solution)/shard_map/all_to_all | solution.py:230
  28.4 0.4 collective-permute-start
  28.9 0.0 slice-done
  28.9 0.0 slice-done.1
  28.9 0.0 slice-done.2
  28.9 0.0 slice-done.3
  28.9 0.0 copy-done
  28.9 2.9 %own_half.1.own_ref = f32[2048,128]{1,0:T(8,128)S(1)} custom-call(f32[128,8,128]{2,1,0:T(8,128)S(1)} %all_to_all.10.recv_ref, s32[1,128]{1,0:T(1,128)S(1)} %bitcast.12, f32[2048,16,128]{2,1,0:T(8,128)S(1)} %bitcast.9), custom_call_target="tpu_custom_call" | custom-call | flops 805306368 | bytes 4194304 | tf_op jit(solution)/shard_map/own_half/pallas_call | solution.py:184
  31.8 0.0 collective-permute-done.swapped_ref
  31.9 3.1 %other_half.1 = f32[32,8,1024]{2,1,0:T(8,128)S(1)} custom-call(f32[128,8,128]{2,1,0:T(8,128)S(1)} %collective-permute-done.swapped_ref, s32[1,128]{1,0:T(1,128)S(1)} %bitcast.13, f32[2048,16,128]{2,1,0:T(8,128)S(1)} %bitcast.10, f32[2048,128]{1,0:T(8,128)S(1)} %own_half.1.own_ref), custom_call_target="tpu_custom_call" | custom-call | tf_op jit(solution)/shard_map/other_half/pallas_call | solution.py:195
  35.0 22.6 %all_to_all.11.parts_ref = f32[32,8,1024]{2,1,0:T(8,128)S(1)} all-to-all(f32[32,8,1024]{2,1,0:T(8,128)S(1)} %other_half.1), channel_id=1, replica_groups=mesh['row'=4,'feat'=32] {'feat'}, dimensions={0} | all-to-all | bytes 2097152 | tf_op jit(solution)/shard_map/all_to_all | solution.py:233
  57.6 0.7 %sum_parts.1 = f32[4,2048]{1,0:T(4,128)} custom-call(f32[32,8,1024]{2,1,0:T(8,128)S(1)} %all_to_all.11.parts_ref), custom_call_target="tpu_custom_call" | custom-call | tf_op jit(solution)/shard_map/sum_parts/pallas_call | solution.py:217
  (1 shorter events, 0.0 us)
Async XLA Ops:
  0.0 4.1 %copy-start.2 = (f32[4,128,128]{2,1,0:T(8,128)S(1)}, f32[4,128,128]{2,1,0:T(8,128)}, u32[]{:S(2)}) copy-start(f32[4,128,128]{2,1,0:T(8,128)} %iout.1) | copy-start | bytes 786436
  0.0 4.1 %copy-start.1 = (f32[4,128,128]{2,1,0:T(8,128)S(1)}, f32[4,128,128]{2,1,0:T(8,128)}, u32[]{:S(2)}) copy-start(f32[4,128,128]{2,1,0:T(8,128)} %iin.1) | copy-start | bytes 786436
  4.1 24.8 %slice-start = ((s8[16777216]{0:T(1024)(128)(4,1)}), s8[4194304]{0:T(1024)(128)(4,1)S(1)}, s32[]{:S(2)}) async-start(s8[16777216]{0:T(1024)(128)(4,1)} %bitcast.7), calls=%async_computation.2 | async-start | bytes 8388608
  4.1 24.7 %slice-start.1 = ((s8[16777216]{0:T(1024)(128)(4,1)}), s8[4194304]{0:T(1024)(128)(4,1)S(1)}, s32[]{:S(2)}) async-start(s8[16777216]{0:T(1024)(128)(4,1)} %bitcast.7), calls=%async_computation.3 | async-start | bytes 8388608
  4.1 24.7 %slice-start.2 = ((s8[16777216]{0:T(1024)(128)(4,1)}), s8[4194304]{0:T(1024)(128)(4,1)S(1)}, s32[]{:S(2)}) async-start(s8[16777216]{0:T(1024)(128)(4,1)} %bitcast.7), calls=%async_computation.4 | async-start | bytes 8388608
  4.1 24.7 %slice-start.3 = ((s8[16777216]{0:T(1024)(128)(4,1)}), s8[4194304]{0:T(1024)(128)(4,1)S(1)}, s32[]{:S(2)}) async-start(s8[16777216]{0:T(1024)(128)(4,1)} %bitcast.7), calls=%async_computation.5 | async-start | bytes 8388608
  4.2 24.7 %copy-start = (s32[128]{0:T(128)S(1)}, s32[128]{0:T(128)}, u32[]{:S(2)}) copy-start(s32[128]{0:T(128)} %param.15) | copy-start | bytes 1540
  28.4 3.4 %collective-permute-start = (f32[128,8,128]{2,1,0:T(8,128)S(1)}, f32[128,8,128]{2,1,0:T(8,128)S(1)}, u32[]{:S(2)}, u32[]{:S(2)}) collective-permute-start(f32[128,8,128]{2,1,0:T(8,128)S(1)} %all_to_all.10.recv_ref), channel_id=1, source_target_pairs={{0,32},{32,0},{64,96},{96,64},{1,33},{33,1},{65,97},{97,65},{2,34}... | collective-permute-start | bytes 1572872 | tf_op jit(solution)/shard_map/ppermute | solution.py:231
